TPU v7x, 512 devices: a whole 4x8x8 slice. The times are simulated.
512 devices in a mesh: mesh: 128 (over y, z, core), sub: 4 (over x).
Axes of the slice: x: 4, y: 8, z: 8, core: 2. Of those that a mesh axis runs over, the one named last changes fastest.
Arguments:
- disp: float32 [3, 2097152], P(None, ('mesh', 'sub')), may hold values from -6 to 6
- velo: float32 [3, 2097152], P(None, ('mesh', 'sub')), may hold values from -6 to 6
- inv_mass: float32 [2097152], P(('mesh', 'sub')), may hold values from 0.05 to 0.2
- hex_nodes: int32 [8, 1048576], P(None, ('mesh', 'sub')), may hold values from -1024 to 5119, as said below
- modulus: float32 [1048576], P(('mesh', 'sub')), may hold values from 0.5 to 2
- yielded: int32 [1048576], P(('mesh', 'sub')), may hold values 0 or 1
- stiffness: float32 [24, 24], replicated
- send_slots: int32 [65536, 32], P(('mesh', 'sub')), may hold values from 0 to 4095, as said below
- fine_slot: int32 [2097152], P(('mesh', 'sub')), may hold values from 0 to 4095, as said below
- fine_disp: float32 [3, 2097152], P(None, ('mesh', 'sub')), may hold values from -6 to 6
- fine_velo: float32 [3, 2097152], P(None, ('mesh', 'sub')), may hold values from -6 to 6
- fine_inv_mass: float32 [2097152], P(('mesh', 'sub')), may hold values from 0.5 to 2
- fine_stiff: float32 [2097152], P(('mesh', 'sub')), may hold values from 0.25 to 1
- tie_stiff: float32 [2097152], P(('mesh', 'sub')), may hold values from 0.25 to 1
Outputs:
- disp_new: float32 [3, 2097152], P(None, ('mesh', 'sub'))
- velo_new: float32 [3, 2097152], P(None, ('mesh', 'sub'))
- fine_pos: float32 [3, 2097152], P(None, ('mesh', 'sub'))
- fine_vel: float32 [3, 2097152], P(None, ('mesh', 'sub'))
Inputs may be any that keep to these rules, and one draw needn't show every extreme that they name: `hex_nodes`: each offset names a node among the device's 4096 nodes or the 1024 nodes on either side of them, and always a node of the whole mesh. `send_slots`: every slot holds a local node number of its owner. `fine_slot`: each helper's 4096 entries are a permutation of 0 to 4095.
All inputs are finite; a program needn't handle non-finite values. No bound on the sum of `yielded` on one device may be relied on, other than what follows from the above.
Results may differ from a plain program's by a relative error of at most 0.00027.
Values sent between devices are 32-bit elements; how exact they have to be, the bound alone decides.
A program may use at most 64 MiB of HBM per device.

v0:
```python
import jax
import jax.numpy as jnp
from jax import lax
from jax.sharding import PartitionSpec as P

SUBSTEPS = 8
GHOST = 1024


DT_FINE = 0.5
DT_COARSE = 1.0
PLASTIC = 0.3


def with_halo(shard, sides, width):
    for axis, dim in sides:
        peers, length = (lax.axis_size(axis), shard.shape[dim])
        up = [(i, (i + 1) % peers) for i in range(peers - 1)]
        down = [(j, i) for i, j in up]
        last = lax.slice_in_dim(shard, length - width, length, axis=dim)
        initial = lax.slice_in_dim(shard, 0, width, axis=dim)
        before = lax.ppermute(last, axis, up)
        after = lax.ppermute(initial, axis, down)
        shard = jnp.concatenate([before, shard, after], axis=dim)
    return shard


def substep_update(fine_pos, fine_vel, padded, attached, fine_inv_mass, fine_stiff, tie_stiff):
    laplace = padded[:, 2:] - 2.0 * fine_pos + padded[:, :-2]
    accel = fine_inv_mass * (fine_stiff * laplace + tie_stiff * (attached - fine_pos))
    fine_vel = fine_vel + DT_FINE * accel
    fine_pos = fine_pos + DT_FINE * fine_vel
    return (fine_pos, fine_vel)


def on_device(
    disp,
    velo,
    inv_mass,
    hex_nodes,
    modulus,
    yielded,
    stiffness,
    send_slots,
    fine_slot,
    fine_disp,
    fine_velo,
    fine_inv_mass,
    fine_stiff,
    tie_stiff,
):
    node_count = disp.shape[1]
    elem_count = hex_nodes.shape[1]
    mesh_count = send_slots.shape[0]
    slot_cap = send_slots.shape[1]
    hex_local = hex_nodes + GHOST
    slot_index = send_slots.reshape(-1)
    picked = jnp.take(disp, slot_index, axis=1).reshape(3, mesh_count, slot_cap)
    received = lax.all_to_all(picked, "mesh", split_axis=1, concat_axis=1, tiled=True)
    attached = jnp.take(received.reshape(3, mesh_count * slot_cap), fine_slot, axis=1)
    extended = with_halo(disp, ((("mesh", "sub"), 1),), GHOST)
    corner = jnp.take(extended, hex_local, axis=1).reshape(24, elem_count)
    factor = modulus * jnp.where(yielded == 1, PLASTIC, 1.0)
    element = (jnp.dot(stiffness, corner, precision=lax.Precision.HIGHEST) * factor).reshape(
        3, 8, elem_count
    )
    ext_force = jnp.zeros((3, node_count + 2 * GHOST), jnp.float32).at[:, hex_local].add(element)
    rims = jnp.concatenate([ext_force[:, :GHOST], ext_force[:, node_count + GHOST :]], axis=1)
    neighbour = with_halo(rims, ((("mesh", "sub"), 1),), GHOST)
    internal = ext_force[:, GHOST : GHOST + node_count]
    internal = internal.at[:, :GHOST].add(neighbour[:, :GHOST])
    internal = internal.at[:, node_count - GHOST :].add(neighbour[:, 3 * GHOST :])
    fine_pos = fine_disp
    fine_vel = fine_velo
    total = jnp.zeros_like(fine_pos)
    for substep in range(SUBSTEPS):
        padded = with_halo(fine_pos, ((("mesh", "sub"), 1),), 1)
        fine_pos, fine_vel = substep_update(
            fine_pos, fine_vel, padded, attached, fine_inv_mass, fine_stiff, tie_stiff
        )
        total = total + fine_pos
    tie_force = tie_stiff * (total * (1.0 / SUBSTEPS) - attached)
    outgoing = jnp.zeros((3, mesh_count * slot_cap), jnp.float32).at[:, fine_slot].set(tie_force)
    returned = lax.all_to_all(
        outgoing.reshape(3, mesh_count, slot_cap), "mesh", split_axis=1, concat_axis=1, tiled=True
    )
    returned = returned.reshape(3, -1)
    coupling = jnp.zeros((3, node_count), jnp.float32).at[:, slot_index].add(returned)
    velo_new = velo + DT_COARSE * (inv_mass * (coupling - internal))
    disp_new = disp + DT_COARSE * velo_new
    return (disp_new, velo_new, fine_pos, fine_vel)


def solution(mesh):
    placed = (
        P(None, ("mesh", "sub")),
        P(None, ("mesh", "sub")),
        P(("mesh", "sub")),
        P(None, ("mesh", "sub")),
        P(("mesh", "sub")),
        P(("mesh", "sub")),
        P(),
        P(("mesh", "sub"), None),
        P(("mesh", "sub")),
        P(None, ("mesh", "sub")),
        P(None, ("mesh", "sub")),
        P(("mesh", "sub")),
        P(("mesh", "sub")),
        P(("mesh", "sub")),
    )
    return jax.shard_map(
        on_device,
        mesh=mesh,
        in_specs=placed,
        out_specs=(
            P(None, ("mesh", "sub")),
            P(None, ("mesh", "sub")),
            P(None, ("mesh", "sub")),
            P(None, ("mesh", "sub")),
        ),
        check_vma=False,
    )
```

profile of v0, /device:TPU:1, one launch (start us, length us, event | category | flops | bytes accessed | tf_op | source)
XLA Modules:
  0.0 427.5 jit_solution(4150945550418713229)
XLA Ops:
  3.1 14.2 %gather_fusion.1 = f32[4096,3]{1,0:T(8,128)} fusion(f32[3,4096]{0,1:T(8,128)S(1)} %copy.329, s32[4096]{0:T(1024)S(1)} %fusion.80), kind=kCustom, calls=%fused_computation.clone | custom fusion | bytes 114688 | tf_op jit(solution)/shard_map/jit(_take)/gather | solution.py:58
  17.3 4.7 %broadcast_select_fusion = f32[4096,3]{1,0:T(8,128)} fusion(f32[4096,3]{1,0:T(8,128)} %gather_fusion.1, pred[4096]{0:T(1024)(128)(4,1)S(1)} %compare_and_fusion.2), kind=kLoop, calls=%fused_computation.11 | loop fusion | flops 12288 | bytes 102400 | tf_op jit(solution)/shard_map/jit(_take)/select_n | solution.py:58
  25.2 18.4 %all-to-all-start = ((f32[3,128,32]{2,0,1:T(4,128)}), f32[3,128,32]{2,0,1:T(4,128)S(1)}, u32[]{:S(2)}, u32[]{:S(2)}) async-start(f32[3,128,32]{2,0,1:T(4,128)} %copy.318), calls=%async_computation | async-start | bytes 524288 | tf_op jit(solution)/shard_map/all_to_all | solution.py:59
  45.0 5.2 %collective-permute-start = (f32[3,1]{1,0:T(4,128)}, f32[3,1]{1,0:T(4,128)S(1)}, u32[]{:S(2)}, u32[]{:S(2)}) collective-permute-start(f32[3,1]{1,0:T(4,128)} %get-tuple-element.78), channel_id=1, source_target_pairs={{1,0},{2,1},{3,2},{4,3},{5,4},{6,5},{7,6},{8,7},{9,8},{10,9},{11,1... | collective-permute-start | bytes 44 | tf_op jit(solution)/shard_map/ppermute | solution.py:23
  54.0 4.9 %collective-permute-start.17 = (f32[3,1024]{1,0:T(4,128)S(1)}, f32[3,1024]{1,0:T(4,128)S(1)}, u32[]{:S(2)}, u32[]{:S(2)}) collective-permute-start(f32[3,1024]{1,0:T(4,128)S(1)} %get-tuple-element.63), channel_id=1, source_target_pairs={{1,0},{2,1},{3,2},{4,3},{5,4},{6,5},{7,6},{8,7},{9,8},{10,9},{11,1... | collective-permute-start | bytes 36872 | tf_op jit(solution)/shard_map/ppermute | solution.py:23
  63.3 60.0 %gather_fusion = f32[16384,3]{1,0:T(8,128)} fusion(f32[3,6144]{0,1:T(8,128)S(1)} %copy.325, s32[16384]{0:T(1024)} %broadcast_clamp_fusion), kind=kCustom, calls=%fused_computation.2 | custom fusion | bytes 458752 | tf_op jit(solution)/shard_map/jit(_take)/gather | solution.py:62
  123.2 5.3 %copy.326 = f32[8,2048,3]{1,0,2:T(8,128)S(1)} copy(f32[8,2048,3]{2,1,0:T(8,128)} %bitcast.92) | data formatting | bytes 393216 | tf_op jit(solution)/shard_map/jit(_take)/gather | solution.py:62
  128.8 4.6 %copy.327 = f32[8,2048,3]{2,1,0:T(8,128)} copy(f32[8,2048,3]{1,0,2:T(8,128)S(1)} %fusion) | data formatting | bytes 393216 | tf_op jit(solution)/shard_map/reshape | solution.py:64
  133.5 88.4 %scatter_custom_fusion.2 = f32[3,6144]{0,1:T(8,128)S(1)} fusion(s32[16384]{0:T(1024)} %bitcast.98, f32[16384,3]{1,0:T(8,128)} %bitcast.95, f32[]{:T(128)} %constant.89.clone.1), kind=kCustom, calls=%fused_computation.9 | custom fusion | flops 49152 | bytes 74240 | tf_op jit(solution)/shard_map/scatter-add | solution.py:67
  229.0 4.8 %collective-permute-start.19 = (f32[3,1024]{0,1:T(8,128)}, f32[3,1024]{0,1:T(8,128)}, u32[]{:S(2)}, u32[]{:S(2)}) collective-permute-start(f32[3,1024]{0,1:T(8,128)} %get-tuple-element.60), channel_id=1, source_target_pairs={{1,0},{2,1},{3,2},{4,3},{5,4},{6,5},{7,6},{8,7},{9,8},{10,9},{11,1... | collective-permute-start | bytes 36872 | tf_op jit(solution)/shard_map/ppermute | solution.py:23
  240.0 14.2 %gather_fusion.2 = f32[4096,3]{1,0:T(8,128)} fusion(f32[3,4096]{0,1:T(8,128)S(1)} %bitcast.96, s32[4096]{0:T(1024)S(1)} %get-tuple-element.80), kind=kCustom, calls=%fused_computation.1.clone | custom fusion | bytes 114688 | tf_op jit(solution)/shard_map/jit(_take)/gather | solution.py:60
  257.4 6.8 %collective-permute-start.2 = (f32[3,1]{1,0:T(4,128)S(1)}, f32[3,1]{1,0:T(4,128)S(1)}, u32[]{:S(2)}, u32[]{:S(2)}) collective-permute-start(f32[3,1]{1,0:T(4,128)S(1)} %get-tuple-element.76), channel_id=1, source_target_pairs={{1,0},{2,1},{3,2},{4,3},{5,4},{6,5},{7,6},{8,7},{9,8},{10,9},{11,1... | collective-permute-start | bytes 44 | tf_op jit(solution)/shard_map/ppermute | solution.py:23
  266.1 4.2 collective-permute-done.3
  273.2 3.3 collective-permute-start.5
  281.5 3.3 collective-permute-start.7
  289.8 3.3 collective-permute-start.9
  298.1 3.3 collective-permute-start.11
  306.5 3.3 collective-permute-start.13
  314.8 3.5 collective-permute-start.15
  323.8 11.4 %scatter_custom_fusion = f32[3,4096]{0,1:T(8,128)S(1)} fusion(s32[4096]{0:T(1024)} %get-tuple-element.81, f32[4096,3]{1,0:T(8,128)} %copy.321, f32[]{:T(128)} %constant.89.clone.1), kind=kCustom, calls=%fused_computation.14 | custom fusion | bytes 49664 | tf_op jit(solution)/shard_map/scatter | solution.py:83
  336.8 41.5 %all-to-all-start.1 = ((f32[3,128,32]{2,0,1:T(4,128)}), f32[3,128,32]{2,0,1:T(4,128)S(1)}, u32[]{:S(2)}, u32[]{:S(2)}) async-start(f32[3,128,32]{2,0,1:T(4,128)} %copy.322), calls=%async_computation.1 | async-start | bytes 524288 | tf_op jit(solution)/shard_map/all_to_all | solution.py:84
  380.4 12.2 %all-to-all-done.1 = f32[3,128,32]{2,0,1:T(4,128)S(1)} async-done(((f32[3,128,32]{2,0,1:T(4,128)}), f32[3,128,32]{2,0,1:T(4,128)S(1)}, u32[]{:S(2)}, u32[]{:S(2)}) %all-to-all-start.1) | async-done | bytes 49184 | tf_op jit(solution)/shard_map/all_to_all | solution.py:84
  394.7 24.1 %scatter_custom_fusion.1 = f32[3,4096]{0,1:T(8,128)} fusion(s32[4096]{0:T(1024)} %bitcast.100, f32[4096,3]{1,0:T(8,128)} %copy.324, f32[]{:T(128)} %constant.89.clone.1), kind=kCustom, calls=%fused_computation.12 | custom fusion | flops 12288 | bytes 49664 | tf_op jit(solution)/shard_map/scatter-add | solution.py:88
  418.8 4.5 %fusion.82 = (f32[3,4096]{0,1:T(8,128)}, f32[3,4096]{0,1:T(8,128)}) fusion(f32[3,4096]{0,1:T(8,128)S(1)} %copy-done.2, f32[3,4096]{0,1:T(8,128)} %copy.328, f32[3,4096]{0,1:T(8,128)} %scatter_custom_fusion.1, f32[3,4096]{0,1:T(8,128)} %fusion.8, f32[4096]{0:T(1024)S(1)} %copy-done.16), kind=kLoop, calls=%fused_computation.139 | loop fusion | flops 49152 | bytes 311296 | tf_op jit(solution)/shard_map/add | solution.py:90
  (118 shorter events, 76.9 us)
Async XLA Ops:
  0.6 127.9 %copy-start = (f32[24,24]{1,0:T(8,128)S(1)}, f32[24,24]{1,0:T(8,128)}, u32[]{:S(2)}) copy-start(f32[24,24]{1,0:T(8,128)} %param.26) | copy-start | bytes 6916
  25.2 214.0 %all-to-all-start = ((f32[3,128,32]{2,0,1:T(4,128)}), f32[3,128,32]{2,0,1:T(4,128)S(1)}, u32[]{:S(2)}, u32[]{:S(2)}) async-start(f32[3,128,32]{2,0,1:T(4,128)} %copy.318), calls=%async_computation | async-start | bytes 524288 | tf_op jit(solution)/shard_map/all_to_all | solution.py:59
  45.0 211.4 %collective-permute-start = (f32[3,1]{1,0:T(4,128)}, f32[3,1]{1,0:T(4,128)S(1)}, u32[]{:S(2)}, u32[]{:S(2)}) collective-permute-start(f32[3,1]{1,0:T(4,128)} %get-tuple-element.78), channel_id=1, source_target_pairs={{1,0},{2,1},{3,2},{4,3},{5,4},{6,5},{7,6},{8,7},{9,8},{10,9},{11,1... | collective-permute-start | bytes 44 | tf_op jit(solution)/shard_map/ppermute | solution.py:23
  50.1 206.3 %collective-permute-start.1 = (f32[3,1]{1,0:T(4,128)}, f32[3,1]{1,0:T(4,128)}, u32[]{:S(2)}, u32[]{:S(2)}) collective-permute-start(f32[3,1]{1,0:T(4,128)} %get-tuple-element.79), channel_id=1, source_target_pairs={{0,1},{1,2},{2,3},{3,4},{4,5},{5,6},{6,7},{7,8},{8,9},{9,10},{10,1... | collective-permute-start | bytes 44 | tf_op jit(solution)/shard_map/ppermute | solution.py:22
  52.1 10.1 %collective-permute-start.16 = (f32[3,1024]{1,0:T(4,128)S(1)}, f32[3,1024]{1,0:T(4,128)S(1)}, u32[]{:S(2)}, u32[]{:S(2)}) collective-permute-start(f32[3,1024]{1,0:T(4,128)S(1)} %get-tuple-element.62), channel_id=1, source_target_pairs={{0,1},{1,2},{2,3},{3,4},{4,5},{5,6},{6,7},{7,8},{8,9},{9,10},{10,1... | collective-permute-start | bytes 36872 | tf_op jit(solution)/shard_map/ppermute | solution.py:22
  54.0 8.1 %collective-permute-start.17 = (f32[3,1024]{1,0:T(4,128)S(1)}, f32[3,1024]{1,0:T(4,128)S(1)}, u32[]{:S(2)}, u32[]{:S(2)}) collective-permute-start(f32[3,1024]{1,0:T(4,128)S(1)} %get-tuple-element.63), channel_id=1, source_target_pairs={{1,0},{2,1},{3,2},{4,3},{5,4},{6,5},{7,6},{8,7},{9,8},{10,9},{11,1... | collective-permute-start | bytes 36872 | tf_op jit(solution)/shard_map/ppermute | solution.py:23
  133.5 91.4 %copy-start.12 = (f32[3,4096]{1,0:T(4,128)S(1)}, f32[3,4096]{1,0:T(4,128)}, u32[]{:S(2)}) copy-start(f32[3,4096]{1,0:T(4,128)} %param.21) | copy-start | bytes 147460
  223.0 13.6 %collective-permute-start.18 = (f32[3,1024]{0,1:T(8,128)}, f32[3,1024]{0,1:T(8,128)}, u32[]{:S(2)}, u32[]{:S(2)}) collective-permute-start(f32[3,1024]{0,1:T(8,128)} %get-tuple-element.61), channel_id=1, source_target_pairs={{0,1},{1,2},{2,3},{3,4},{4,5},{5,6},{6,7},{7,8},{8,9},{9,10},{10,1... | collective-permute-start | bytes 36872 | tf_op jit(solution)/shard_map/ppermute | solution.py:22
  229.0 149.3 %collective-permute-start.19 = (f32[3,1024]{0,1:T(8,128)}, f32[3,1024]{0,1:T(8,128)}, u32[]{:S(2)}, u32[]{:S(2)}) collective-permute-start(f32[3,1024]{0,1:T(8,128)} %get-tuple-element.60), channel_id=1, source_target_pairs={{1,0},{2,1},{3,2},{4,3},{5,4},{6,5},{7,6},{8,7},{9,8},{10,9},{11,1... | collective-permute-start | bytes 36872 | tf_op jit(solution)/shard_map/ppermute | solution.py:23
  257.4 8.7 %collective-permute-start.2 = (f32[3,1]{1,0:T(4,128)S(1)}, f32[3,1]{1,0:T(4,128)S(1)}, u32[]{:S(2)}, u32[]{:S(2)}) collective-permute-start(f32[3,1]{1,0:T(4,128)S(1)} %get-tuple-element.76), channel_id=1, source_target_pairs={{1,0},{2,1},{3,2},{4,3},{5,4},{6,5},{7,6},{8,7},{9,8},{10,9},{11,1... | collective-permute-start | bytes 44 | tf_op jit(solution)/shard_map/ppermute | solution.py:23
  264.2 6.1 %collective-permute-start.3 = (f32[3,1]{1,0:T(4,128)S(1)}, f32[3,1]{1,0:T(4,128)S(1)}, u32[]{:S(2)}, u32[]{:S(2)}) collective-permute-start(f32[3,1]{1,0:T(4,128)S(1)} %get-tuple-element.77), channel_id=1, source_target_pairs={{0,1},{1,2},{2,3},{3,4},{4,5},{5,6},{6,7},{7,8},{8,9},{9,10},{10,1... | collective-permute-start | bytes 44 | tf_op jit(solution)/shard_map/ppermute | solution.py:22
  271.2 5.3 %collective-permute-start.4 = (f32[3,1]{1,0:T(4,128)S(1)}, f32[3,1]{1,0:T(4,128)S(1)}, u32[]{:S(2)}, u32[]{:S(2)}) collective-permute-start(f32[3,1]{1,0:T(4,128)S(1)} %get-tuple-element.74), channel_id=1, source_target_pairs={{1,0},{2,1},{3,2},{4,3},{5,4},{6,5},{7,6},{8,7},{9,8},{10,9},{11,1... | collective-permute-start | bytes 44 | tf_op jit(solution)/shard_map/ppermute | solution.py:23
  273.2 6.1 %collective-permute-start.5 = (f32[3,1]{1,0:T(4,128)S(1)}, f32[3,1]{1,0:T(4,128)S(1)}, u32[]{:S(2)}, u32[]{:S(2)}) collective-permute-start(f32[3,1]{1,0:T(4,128)S(1)} %get-tuple-element.75), channel_id=1, source_target_pairs={{0,1},{1,2},{2,3},{3,4},{4,5},{5,6},{6,7},{7,8},{8,9},{9,10},{10,1... | collective-permute-start | bytes 44 | tf_op jit(solution)/shard_map/ppermute | solution.py:22
  279.5 5.3 %collective-permute-start.6 = (f32[3,1]{1,0:T(4,128)S(1)}, f32[3,1]{1,0:T(4,128)S(1)}, u32[]{:S(2)}, u32[]{:S(2)}) collective-permute-start(f32[3,1]{1,0:T(4,128)S(1)} %get-tuple-element.72), channel_id=1, source_target_pairs={{1,0},{2,1},{3,2},{4,3},{5,4},{6,5},{7,6},{8,7},{9,8},{10,9},{11,1... | collective-permute-start | bytes 44 | tf_op jit(solution)/shard_map/ppermute | solution.py:23
  281.5 6.1 %collective-permute-start.7 = (f32[3,1]{1,0:T(4,128)S(1)}, f32[3,1]{1,0:T(4,128)S(1)}, u32[]{:S(2)}, u32[]{:S(2)}) collective-permute-start(f32[3,1]{1,0:T(4,128)S(1)} %get-tuple-element.73), channel_id=1, source_target_pairs={{0,1},{1,2},{2,3},{3,4},{4,5},{5,6},{6,7},{7,8},{8,9},{9,10},{10,1... | collective-permute-start | bytes 44 | tf_op jit(solution)/shard_map/ppermute | solution.py:22
  287.9 5.3 %collective-permute-start.8 = (f32[3,1]{1,0:T(4,128)S(1)}, f32[3,1]{1,0:T(4,128)S(1)}, u32[]{:S(2)}, u32[]{:S(2)}) collective-permute-start(f32[3,1]{1,0:T(4,128)S(1)} %get-tuple-element.70), channel_id=1, source_target_pairs={{1,0},{2,1},{3,2},{4,3},{5,4},{6,5},{7,6},{8,7},{9,8},{10,9},{11,1... | collective-permute-start | bytes 44 | tf_op jit(solution)/shard_map/ppermute | solution.py:23
  289.8 6.1 %collective-permute-start.9 = (f32[3,1]{1,0:T(4,128)S(1)}, f32[3,1]{1,0:T(4,128)S(1)}, u32[]{:S(2)}, u32[]{:S(2)}) collective-permute-start(f32[3,1]{1,0:T(4,128)S(1)} %get-tuple-element.71), channel_id=1, source_target_pairs={{0,1},{1,2},{2,3},{3,4},{4,5},{5,6},{6,7},{7,8},{8,9},{9,10},{10,1... | collective-permute-start | bytes 44 | tf_op jit(solution)/shard_map/ppermute | solution.py:22
  296.2 5.3 %collective-permute-start.10 = (f32[3,1]{1,0:T(4,128)S(1)}, f32[3,1]{1,0:T(4,128)S(1)}, u32[]{:S(2)}, u32[]{:S(2)}) collective-permute-start(f32[3,1]{1,0:T(4,128)S(1)} %get-tuple-element.68), channel_id=1, source_target_pairs={{1,0},{2,1},{3,2},{4,3},{5,4},{6,5},{7,6},{8,7},{9,8},{10,9},{11,1... | collective-permute-start | bytes 44 | tf_op jit(solution)/shard_map/ppermute | solution.py:23
  298.1 6.1 %collective-permute-start.11 = (f32[3,1]{1,0:T(4,128)S(1)}, f32[3,1]{1,0:T(4,128)S(1)}, u32[]{:S(2)}, u32[]{:S(2)}) collective-permute-start(f32[3,1]{1,0:T(4,128)S(1)} %get-tuple-element.69), channel_id=1, source_target_pairs={{0,1},{1,2},{2,3},{3,4},{4,5},{5,6},{6,7},{7,8},{8,9},{9,10},{10,1... | collective-permute-start | bytes 44 | tf_op jit(solution)/shard_map/ppermute | solution.py:22
  304.6 5.3 %collective-permute-start.12 = (f32[3,1]{1,0:T(4,128)S(1)}, f32[3,1]{1,0:T(4,128)S(1)}, u32[]{:S(2)}, u32[]{:S(2)}) collective-permute-start(f32[3,1]{1,0:T(4,128)S(1)} %get-tuple-element.66), channel_id=1, source_target_pairs={{1,0},{2,1},{3,2},{4,3},{5,4},{6,5},{7,6},{8,7},{9,8},{10,9},{11,1... | collective-permute-start | bytes 44 | tf_op jit(solution)/shard_map/ppermute | solution.py:23
  306.5 6.1 %collective-permute-start.13 = (f32[3,1]{1,0:T(4,128)S(1)}, f32[3,1]{1,0:T(4,128)S(1)}, u32[]{:S(2)}, u32[]{:S(2)}) collective-permute-start(f32[3,1]{1,0:T(4,128)S(1)} %get-tuple-element.67), channel_id=1, source_target_pairs={{0,1},{1,2},{2,3},{3,4},{4,5},{5,6},{6,7},{7,8},{8,9},{9,10},{10,1... | collective-permute-start | bytes 44 | tf_op jit(solution)/shard_map/ppermute | solution.py:22
  312.8 5.5 %collective-permute-start.14 = (f32[3,1]{1,0:T(4,128)S(1)}, f32[3,1]{1,0:T(4,128)S(1)}, u32[]{:S(2)}, u32[]{:S(2)}) collective-permute-start(f32[3,1]{1,0:T(4,128)S(1)} %get-tuple-element.64), channel_id=1, source_target_pairs={{1,0},{2,1},{3,2},{4,3},{5,4},{6,5},{7,6},{8,7},{9,8},{10,9},{11,1... | collective-permute-start | bytes 44 | tf_op jit(solution)/shard_map/ppermute | solution.py:23
  314.8 6.1 %collective-permute-start.15 = (f32[3,1]{1,0:T(4,128)S(1)}, f32[3,1]{1,0:T(4,128)S(1)}, u32[]{:S(2)}, u32[]{:S(2)}) collective-permute-start(f32[3,1]{1,0:T(4,128)S(1)} %get-tuple-element.65), channel_id=1, source_target_pairs={{0,1},{1,2},{2,3},{3,4},{4,5},{5,6},{6,7},{7,8},{8,9},{9,10},{10,1... | collective-permute-start | bytes 44 | tf_op jit(solution)/shard_map/ppermute | solution.py:22
  336.8 55.7 %all-to-all-start.1 = ((f32[3,128,32]{2,0,1:T(4,128)}), f32[3,128,32]{2,0,1:T(4,128)S(1)}, u32[]{:S(2)}, u32[]{:S(2)}) async-start(f32[3,128,32]{2,0,1:T(4,128)} %copy.322), calls=%async_computation.1 | async-start | bytes 524288 | tf_op jit(solution)/shard_map/all_to_all | solution.py:84
  (17 other events, 356.0 us)
where the time goes:
time: 430 us; the launch traced here: 428 us
  local copies, waits for them, and re-layouts  136 us (32%)
  other arithmetic  134 us (31%)
  starting transfers between devices  121 us (28%)
  waiting for transfers between devices  35.5 us (8%)
    scatter-add x1, other arithmetic, on_device(): jnp.zeros((3, node_count + 2 * GHOST), jnp.float32).at[:, hex_local]  88.4 us
    gather x2, local copies, waits for them, and re-layouts, on_device(): corner = jnp.take(extended, hex_local, axis=1).reshape(24, elem_count)  65.2 us
    all_to_all x1, starting transfers between devices, on_device(): lax.all_to_all(outgoing.reshape(3, mesh_count, slot_cap), 'mesh', split_a...  41.5 us
    ppermute x10, starting transfers between devices, with_halo(): after = lax.ppermute(initial, axis, down)  33.3 us
    ppermute x10, starting transfers between devices, with_halo(): before = lax.ppermute(last, axis, up)  27.8 us
    scatter-add x1, other arithmetic, on_device(): jnp.zeros((3, node_count), jnp.float32).at[:, slot_index].add(returned)  24.1 us
    ppermute x10, waiting for transfers between devices, with_halo(): before = lax.ppermute(last, axis, up)  23.3 us
    all_to_all x1, starting transfers between devices, on_device(): lax.all_to_all(picked, 'mesh', split_axis=1, concat_axis=1, tiled=True)  18.4 us
  transfers between devices with their start and end apart: 22, of which 9 were waited for; matrix products, arithmetic and copies ran while one was open for 49% of the time, Pallas kernels for 0%

commit v1 on v0

v1 whole, which is shorter than its diff:
```python
import jax
import jax.numpy as jnp
from jax import lax
from jax.experimental import pallas as pl
from jax.experimental.pallas import tpu as pltpu
from jax.sharding import PartitionSpec as P

SUBSTEPS = 8
DT_FINE = 0.5
DT_COARSE = 1.0
PLASTIC = 0.3

LANES = 128
CAP = 32
PEERS = 128
GROUPS = LANES // CAP
ROWS = 32
RIM = 8
EXT = ROWS + 2 * RIM
ELEMS = 2048
CHUNK = 512
EDGE = 8
MESH = pl.DeviceIdType.MESH
F32 = jnp.float32
BF16 = jnp.bfloat16


def lane_lookup(acc, table_row, rows, row_idx, lane_idx):
    acc = list(acc)
    for r in rows:
        hit = row_idx == r
        for c in range(3):
            entry = jnp.broadcast_to(table_row(c, r), (8, LANES))
            found = jnp.take_along_axis(entry, lane_idx, axis=1, mode="promise_in_bounds")
            acc[c] = jnp.where(hit, found, acc[c])
    return acc


def scatter_terms(height, row_idx, lane_idx, values):
    n = row_idx.shape[1]
    row_hit = row_idx == lax.broadcasted_iota(jnp.int32, (height, n), 0)
    lane_hit = lane_idx == lax.broadcasted_iota(jnp.int32, (LANES, n), 0)
    parts = []
    for v in values:
        upper = v.astype(BF16).astype(F32)
        for part in (upper, v - upper):
            parts.append(jnp.where(row_hit, jnp.broadcast_to(part, (height, n)), 0.0))
    left = jnp.concatenate(parts, axis=0).astype(BF16)
    right = jnp.where(lane_hit, 1.0, 0.0).astype(BF16)
    return lax.dot_general(left, right, (((1,), (1,)), ((), ())), preferred_element_type=F32)


def widen(table, slot_rows):
    return jnp.concatenate([table(g)[:, slot_rows] for g in range(GROUPS)], axis=1)


def split_rows(ref, store):
    for q in range(ROWS):
        for c in range(3):
            store(c, q, ref[c : c + 1, q * LANES : (q + 1) * LANES])


def substeps(pos, vel, total, shifted, attached, inv_mass, stiff, tie):
    for _ in range(SUBSTEPS):
        for c in range(len(pos)):
            before, after = shifted(pos[c])
            laplace = after - 2.0 * pos[c] + before
            accel = inv_mass * (stiff * laplace + tie * (attached[c] - pos[c]))
            vel[c] = vel[c] + DT_FINE * accel
            pos[c] = pos[c] + DT_FINE * vel[c]
            total[c] = total[c] + pos[c]


def exchange_kernel(
    disp,
    hex_nodes,
    modulus,
    yielded,
    stiffness,
    send_slots,
    fine_slot,
    fine_disp,
    fine_velo,
    fine_inv_mass,
    fine_stiff,
    tie_stiff,
    returned,
    internal,
    pos_out,
    vel_out,
    ext,
    corner,
    force,
    force_in,
    picked,
    received,
    table,
    outgoing,
    edge_out,
    edge_in,
    tied_out,
    tied_in,
    a2a_send,
    a2a_recv,
    halo_send,
    halo_recv,
):
    me, sub = lax.axis_index("mesh"), lax.axis_index("sub")
    n_sub = lax.axis_size("sub")
    top = sub == n_sub - 1
    low = sub == 0
    after = (jnp.where(top, lax.rem(me + 1, PEERS), me), jnp.where(top, 0, sub + 1))
    before = (jnp.where(low, lax.rem(me + PEERS - 1, PEERS), me), jnp.where(low, n_sub - 1, sub - 1))

    barrier = pltpu.get_barrier_semaphore()

    def greet(k, carry):
        pl.semaphore_signal(barrier, inc=1, device_id=(lax.rem(me + k, PEERS), sub), device_id_type=MESH)
        return carry

    for neighbour in (before, after):
        pl.semaphore_signal(barrier, inc=1, device_id=neighbour, device_id_type=MESH)
    lax.fori_loop(1, PEERS, greet, 0)

    def to(neighbour, src, dst, which):
        return pltpu.make_async_remote_copy(
            src, dst, halo_send.at[which], halo_recv.at[which], device_id=neighbour, device_id_type=MESH
        )

    def put_disp(c, q, row):
        ext[c, RIM + q : RIM + q + 1, :] = row

    split_rows(disp, put_disp)

    slot_at = widen(lambda g: send_slots[g * CAP : (g + 1) * CAP, :], slice(0, CAP))
    found = []
    for b in range(ROWS // 8):
        at = slot_at[b * 8 : (b + 1) * 8]
        zero = jnp.zeros((8, LANES), F32)
        found.append(
            lane_lookup(
                [zero] * 3, lambda c, r: ext[c, RIM + r : RIM + r + 1, :], range(ROWS), at >> 7, at & (LANES - 1)
            )
        )
    pad = jnp.zeros((ROWS, LANES - 3 * CAP), F32)
    for g in range(GROUPS):
        cut = [jnp.concatenate([f[c] for f in found], axis=0)[:, g * CAP : (g + 1) * CAP] for c in range(3)]
        picked[g * ROWS : (g + 1) * ROWS] = jnp.concatenate(cut + [pad], axis=1).reshape(ROWS, 1, LANES)

    def put_pos(c, q, row):
        pos_out[c, q : q + 1, :] = row

    def put_vel(c, q, row):
        vel_out[c, q : q + 1, :] = row

    split_rows(fine_disp, put_pos)
    split_rows(fine_velo, put_vel)
    for side, q in ((0, 0), (1, ROWS - 1)):
        for c in range(3):
            edge_out[side, c : c + 1, :] = pos_out[c, q : q + 1, :]
            edge_out[side, 3 + c : 4 + c, :] = vel_out[c, q : q + 1, :]
        edge_out[side, 6:7, :] = fine_inv_mass[q : q + 1, :]
        edge_out[side, 7:8, :] = fine_stiff[q : q + 1, :]
        edge_out[side, 8:9, :] = tie_stiff[q : q + 1, :]
        edge_out[side, 9:16, :] = jnp.zeros((7, LANES), F32)

    def own_corner(t, carry):
        cols = pl.ds(pl.multiple_of(t * LANES, LANES), LANES)
        at = hex_nodes[:, cols] + RIM * LANES
        zero = jnp.zeros((8, LANES), F32)
        got = lane_lookup(
            [zero] * 3, lambda c, r: ext[c, r : r + 1, :], range(RIM, RIM + ROWS), at >> 7, at & (LANES - 1)
        )
        for c in range(3):
            corner[c * 8 : (c + 1) * 8, cols] = got[c]
        return carry

    lax.fori_loop(0, ELEMS // LANES, own_corner, 0)

    pl.semaphore_wait(barrier, PEERS + 1)

    halos = [
        to(after, ext.at[:, pl.ds(ROWS, RIM), :], ext.at[:, pl.ds(0, RIM), :], 0),
        to(before, ext.at[:, pl.ds(RIM, RIM), :], ext.at[:, pl.ds(RIM + ROWS, RIM), :], 1),
        to(before, edge_out.at[0], edge_in.at[1], 2),
        to(after, edge_out.at[1], edge_in.at[0], 3),
    ]
    for copy in halos[:2]:
        copy.start()

    def all_to_all(src, dst, which):
        def send(k, carry):
            peer = lax.rem(me + k, PEERS)
            pltpu.make_async_remote_copy(
                src.at[peer],
                dst.at[me],
                a2a_send.at[which],
                a2a_recv.at[which],
                device_id=(peer, sub),
                device_id_type=MESH,
            ).start()
            return carry

        lax.fori_loop(1, PEERS, send, 0)
        dst[pl.ds(me, 1)] = src[pl.ds(me, 1)]
        return pltpu.make_async_remote_copy(
            src.at[pl.ds(0, PEERS - 1)],
            dst.at[pl.ds(0, PEERS - 1)],
            a2a_send.at[which],
            a2a_recv.at[which],
            device_id=after,
            device_id_type=MESH,
        )

    first = all_to_all(picked, received, 0)
    for copy in halos[2:]:
        copy.start()

    force[...] = jnp.zeros_like(force)
    for copy in halos[:2]:
        copy.wait()

    def rim_corner(t, carry):
        cols = pl.ds(pl.multiple_of(t * LANES, LANES), LANES)
        at = hex_nodes[:, cols] + RIM * LANES
        got = lane_lookup(
            [corner[c * 8 : (c + 1) * 8, cols] for c in range(3)],
            lambda c, r: ext[c, r : r + 1, :],
            [*range(RIM), *range(RIM + ROWS, EXT)],
            at >> 7,
            at & (LANES - 1),
        )
        for c in range(3):
            corner[c * 8 : (c + 1) * 8, cols] = got[c]
        return carry

    lax.fori_loop(0, ELEMS // LANES, rim_corner, 0)

    def element_force(t, carry):
        cols = pl.ds(pl.multiple_of(t * CHUNK, CHUNK), CHUNK)
        factor = modulus[:, cols] * jnp.where(yielded[:, cols] == 1, PLASTIC, 1.0)
        element = (
            jnp.dot(stiffness[...], corner[:, cols], precision=lax.Precision.HIGHEST, preferred_element_type=F32)
            * factor
        )
        at = hex_nodes[:, cols] + RIM * LANES
        row_at, lane_at = at >> 7, at & (LANES - 1)
        for k in range(8):
            force[...] += scatter_terms(
                EXT, row_at[k : k + 1], lane_at[k : k + 1], [element[c * 8 + k : c * 8 + k + 1] for c in range(3)]
            )
        return carry

    lax.fori_loop(0, ELEMS // CHUNK, element_force, 0)
    for c in range(3):
        ext_force = force[2 * c * EXT : (2 * c + 1) * EXT, :] + force[(2 * c + 1) * EXT : (2 * c + 2) * EXT, :]
        force[2 * c * EXT : (2 * c + 1) * EXT, :] = ext_force
        force_in[2, c] = ext_force[:RIM]
        force_in[3, c] = ext_force[RIM + ROWS :]
    rims = [
        to(before, force_in.at[2], force_in.at[1], 4),
        to(after, force_in.at[3], force_in.at[0], 5),
    ]
    for copy in rims:
        copy.start()

    first.wait_recv()
    for c in range(3):
        table[c] = widen(lambda g: received[g * ROWS : (g + 1) * ROWS].reshape(ROWS, LANES), slice(c * CAP, (c + 1) * CAP))
    slot = fine_slot[...]
    row_at = (slot >> 5) & (ROWS - 1)
    lane_at = ((slot >> 10) << 5) | (slot & (CAP - 1))
    blocks = []
    for b in range(ROWS // 8):
        zero = jnp.zeros((8, LANES), F32)
        blocks.append(
            lane_lookup(
                [zero] * 3,
                lambda c, r: table[c, r : r + 1, :],
                range(ROWS),
                row_at[b * 8 : (b + 1) * 8],
                lane_at[b * 8 : (b + 1) * 8],
            )
        )
    attached = [jnp.concatenate([b[c] for b in blocks], axis=0) for c in range(3)]
    none = jnp.zeros((5, LANES), F32)
    tied_out[0] = jnp.concatenate([a[:1] for a in attached] + [none], axis=0)
    tied_out[1] = jnp.concatenate([a[ROWS - 1 :] for a in attached] + [none], axis=0)
    ties = [to(before, tied_out.at[0], tied_in.at[1], 6), to(after, tied_out.at[1], tied_in.at[0], 7)]
    for copy in ties:
        copy.start()

    lane = lax.broadcasted_iota(jnp.int32, (ROWS, LANES), 1)

    def shifted(x):
        right = pltpu.roll(x, 1, 1)
        left = pltpu.roll(x, LANES - 1, 1)
        prev = jnp.where(lane == 0, pltpu.roll(right, 1, 0), right)
        nxt = jnp.where(lane == LANES - 1, pltpu.roll(left, ROWS - 1, 0), left)
        return prev, nxt

    pos = [pos_out[c] for c in range(3)]
    vel = [vel_out[c] for c in range(3)]
    total = [jnp.zeros((ROWS, LANES), F32) for _ in range(3)]
    im, st, tie = fine_inv_mass[...], fine_stiff[...], tie_stiff[...]
    first_rows = [x[:1] for x in pos + vel + [im, st, tie] + attached]
    last_rows = [x[ROWS - 1 :] for x in pos + vel + [im, st, tie] + attached]
    substeps(pos, vel, total, shifted, attached, im, st, tie)

    for copy in halos[2:] + ties:
        copy.wait()
    strip_lane = lax.broadcasted_iota(jnp.int32, (1, LANES), 1)
    starts = (me == 0) & (sub == 0)
    ends = (me == PEERS - 1) & (sub == n_sub - 1)

    def head(row, ghost):
        ghost = jnp.where(starts, 0.0, pltpu.roll(ghost, EDGE, 1))
        return jnp.where(strip_lane < EDGE, ghost, pltpu.roll(row, EDGE, 1))

    def tail(row, ghost):
        ghost = jnp.where(ends, 0.0, pltpu.roll(ghost, LANES - EDGE, 1))
        return jnp.where(strip_lane >= LANES - EDGE, ghost, pltpu.roll(row, LANES - EDGE, 1))

    ghost_head = [edge_in[0, i : i + 1, :] for i in range(9)] + [tied_in[0, c : c + 1, :] for c in range(3)]
    ghost_tail = [edge_in[1, i : i + 1, :] for i in range(9)] + [tied_in[1, c : c + 1, :] for c in range(3)]
    heads = [head(r, g) for r, g in zip(first_rows, ghost_head)]
    tails = [tail(r, g) for r, g in zip(last_rows, ghost_tail)]
    blank = jnp.zeros((2, LANES), F32)

    def strip(picks):
        return jnp.concatenate([heads[i] for i in picks] + [tails[i] for i in picks] + [blank], axis=0)

    strip_pos, strip_vel, strip_total = [strip((0, 1, 2))], [strip((3, 4, 5))], [jnp.zeros((8, LANES), F32)]
    substeps(
        strip_pos,
        strip_vel,
        strip_total,
        lambda x: (pltpu.roll(x, 1, 1), pltpu.roll(x, LANES - 1, 1)),
        [strip((9, 10, 11))],
        strip((6, 6, 6)),
        strip((7, 7, 7)),
        strip((8, 8, 8)),
    )
    sub_row = lax.broadcasted_iota(jnp.int32, (ROWS, LANES), 0)
    at_head = (sub_row == 0) & (lane < EDGE)
    at_tail = (sub_row == ROWS - 1) & (lane >= LANES - EDGE)

    def put_ends(whole, strips):
        forward = pltpu.roll(strips, LANES - EDGE, 1)
        back = pltpu.roll(strips, EDGE, 1)
        out = []
        for c in range(3):
            x = jnp.where(at_head, jnp.broadcast_to(forward[c : c + 1], (ROWS, LANES)), whole[c])
            out.append(jnp.where(at_tail, jnp.broadcast_to(back[3 + c : 4 + c], (ROWS, LANES)), x))
        return out

    pos = put_ends(pos, strip_pos[0])
    vel = put_ends(vel, strip_vel[0])
    total = put_ends(total, strip_total[0])
    for c in range(3):
        pos_out[c] = pos[c]
        vel_out[c] = vel[c]

    sums = None
    pull = [tie * (total[c] * (1.0 / SUBSTEPS) - attached[c]) for c in range(3)]
    for q in range(0, ROWS, 4):

        def flat(x):
            return jnp.concatenate([x[q + i : q + i + 1] for i in range(4)], axis=1)

        term = scatter_terms(ROWS, flat(row_at), flat(lane_at), [flat(p) for p in pull])
        sums = term if sums is None else sums + term
    force_at = [sums[2 * c * ROWS : (2 * c + 1) * ROWS] + sums[(2 * c + 1) * ROWS : (2 * c + 2) * ROWS] for c in range(3)]
    for g in range(GROUPS):
        cut = [f[:, g * CAP : (g + 1) * CAP] for f in force_at]
        outgoing[g * ROWS : (g + 1) * ROWS] = jnp.concatenate(cut + [pad], axis=1).reshape(ROWS, 1, LANES)
    second = all_to_all(outgoing, returned, 1)

    for copy in rims:
        copy.wait()
    for c in range(3):
        own = force[2 * c * EXT + RIM : 2 * c * EXT + RIM + ROWS, :]
        internal[c, :RIM] = own[:RIM] + force_in[0, c]
        internal[c, RIM : ROWS - RIM] = own[RIM : ROWS - RIM]
        internal[c, ROWS - RIM :] = own[ROWS - RIM :] + force_in[1, c]
    first.wait_send()
    second.wait()


def update_kernel(
    disp, velo, inv_mass, send_slots, returned, internal, pos, vel, disp_new, velo_new, pos_out, vel_out
):
    slot_at = widen(lambda g: send_slots[g * CAP : (g + 1) * CAP, :], slice(0, CAP))
    back = [
        widen(lambda g: returned[g * ROWS : (g + 1) * ROWS].reshape(ROWS, LANES), slice(c * CAP, (c + 1) * CAP))
        for c in range(3)
    ]
    row_at, lane_at = slot_at >> 7, slot_at & (LANES - 1)
    sums = None
    for q in range(0, ROWS, 4):

        def flat(x):
            return jnp.concatenate([x[q + i : q + i + 1] for i in range(4)], axis=1)

        term = scatter_terms(ROWS, flat(row_at), flat(lane_at), [flat(b) for b in back])
        sums = term if sums is None else sums + term
    change = []
    for c in range(3):
        coupling = sums[2 * c * ROWS : (2 * c + 1) * ROWS] + sums[(2 * c + 1) * ROWS : (2 * c + 2) * ROWS]
        change.append(inv_mass[...] * (coupling - internal[c]))
    for q in range(ROWS):
        cols = slice(q * LANES, (q + 1) * LANES)

        def three(x):
            return jnp.concatenate([x(c) for c in range(3)], axis=0)

        v = velo[:, cols] + DT_COARSE * three(lambda c: change[c][q : q + 1])
        velo_new[:, cols] = v
        disp_new[:, cols] = disp[:, cols] + DT_COARSE * v
        pos_out[:, cols] = three(lambda c: pos[c, q : q + 1, :])
        vel_out[:, cols] = three(lambda c: vel[c, q : q + 1, :])


def on_device(
    disp,
    velo,
    inv_mass,
    hex_nodes,
    modulus,
    yielded,
    stiffness,
    send_slots,
    fine_slot,
    fine_disp,
    fine_velo,
    fine_inv_mass,
    fine_stiff,
    tie_stiff,
):
    vmem = pl.BlockSpec(memory_space=pltpu.VMEM)
    chain = jax.ShapeDtypeStruct((3, ROWS, LANES), F32)
    flat = jax.ShapeDtypeStruct(disp.shape, F32)
    rows = lambda x: x.reshape(ROWS, LANES)
    line = lambda x: x.reshape(1, ELEMS)
    buffer = lambda *shape: pltpu.VMEM(shape, F32)
    returned, internal, pos, vel = pl.pallas_call(
        exchange_kernel,
        out_shape=(jax.ShapeDtypeStruct((PEERS, 1, LANES), F32), chain, chain, chain),
        in_specs=[vmem] * 12,
        out_specs=(vmem,) * 4,
        scratch_shapes=[
            buffer(3, EXT, LANES),
            buffer(24, ELEMS),
            buffer(6 * EXT, LANES),
            buffer(4, 3, RIM, LANES),
            buffer(PEERS, 1, LANES),
            buffer(PEERS, 1, LANES),
            buffer(3, ROWS, LANES),
            buffer(PEERS, 1, LANES),
            buffer(2, 16, LANES),
            buffer(2, 16, LANES),
            buffer(2, 8, LANES),
            buffer(2, 8, LANES),
            pltpu.SemaphoreType.DMA((2,)),
            pltpu.SemaphoreType.DMA((2,)),
            pltpu.SemaphoreType.DMA((8,)),
            pltpu.SemaphoreType.DMA((8,)),
        ],
        compiler_params=pltpu.CompilerParams(
            collective_id=0, has_side_effects=True, vmem_limit_bytes=32 * 1024 * 1024
        ),
        name="exchange",
    )(
        disp,
        hex_nodes,
        line(modulus),
        line(yielded),
        stiffness,
        send_slots,
        rows(fine_slot),
        fine_disp,
        fine_velo,
        rows(fine_inv_mass),
        rows(fine_stiff),
        rows(tie_stiff),
    )
    return pl.pallas_call(
        update_kernel,
        out_shape=(flat,) * 4,
        in_specs=[vmem] * 8,
        out_specs=(vmem,) * 4,
        compiler_params=pltpu.CompilerParams(vmem_limit_bytes=32 * 1024 * 1024),
        name="update",
    )(disp, velo, rows(inv_mass), send_slots, returned, internal, pos, vel)


def solution(mesh):
    placed = (
        P(None, ("mesh", "sub")),
        P(None, ("mesh", "sub")),
        P(("mesh", "sub")),
        P(None, ("mesh", "sub")),
        P(("mesh", "sub")),
        P(("mesh", "sub")),
        P(),
        P(("mesh", "sub"), None),
        P(("mesh", "sub")),
        P(None, ("mesh", "sub")),
        P(None, ("mesh", "sub")),
        P(("mesh", "sub")),
        P(("mesh", "sub")),
        P(("mesh", "sub")),
    )
    return jax.shard_map(
        on_device,
        mesh=mesh,
        in_specs=placed,
        out_specs=(
            P(None, ("mesh", "sub")),
            P(None, ("mesh", "sub")),
            P(None, ("mesh", "sub")),
            P(None, ("mesh", "sub")),
        ),
        check_vma=False,
    )
```

time: 430 us -> 49.1 us (0.11)
  other arithmetic: 134 us -> 0 us
  local copies, waits for them, and re-layouts: 136 us -> 6.92 us
  starting transfers between devices: 121 us -> 0 us
  Pallas kernels: 0 us -> 40.9 us
  waiting for transfers between devices: 35.5 us -> 0 us
    scatter-add x4 -> x0, other arithmetic: 117 us -> none  [the longest x1 88.4 us: on_device(): jnp.zeros((3, node_count + 2 * GHOST), jnp.float32).at[:, hex_local]]
    gather x5 -> x0, local copies, waits for them, and re-layouts: 95.8 us -> none  [the longest x2 65.2 us: on_device(): corner = jnp.take(extended, hex_local, axis=1).reshape(24, elem_count)]
    ppermute x20 -> x0, starting transfers between devices: 61.1 us -> none  [the longest x10 33.3 us: with_halo(): after = lax.ppermute(initial, axis, down)]
    all_to_all x2 -> x0, starting transfers between devices: 59.9 us -> none  [the longest x1 41.5 us: on_device(): lax.all_to_all(outgoing.reshape(3, mesh_count, slot_cap), 'mesh', split_a...]
    pallas_call x0 -> x2, Pallas kernels: none -> 40.9 us  [the longest x1 39.5 us: on_device(): pl.pallas_call(exchange_kernel, out_shape=(jax.ShapeDtypeStruct((PEERS, 1...]
    ppermute x20 -> x0, waiting for transfers between devices: 23.3 us -> none  [the longest x10 23.3 us: with_halo(): before = lax.ppermute(last, axis, up)]
    all_to_all x2 -> x0, waiting for transfers between devices: 12.2 us -> none  [the longest x1 12.2 us: on_device(): lax.all_to_all(outgoing.reshape(3, mesh_count, slot_cap), 'mesh', split_a...]
    reshape x7 -> x0, local copies, waits for them, and re-layouts: 11.7 us -> none  [the longest x1 4.64 us: on_device(): (jnp.dot(stiffness, corner, precision=lax.Precision.HIGHEST) * factor).re...]
  transfers between devices with their start and end apart: 22 -> 0, of which waited for: 9 -> 0; matrix products, arithmetic and copies ran while one was open for 49% -> 0% of each run, Pallas kernels for 0% -> 0%
where the time goes in v1:
time: 49.1 us; the launch traced here: 48.5 us
  Pallas kernels  40.9 us (83%)
  local copies, waits for them, and re-layouts  6.92 us (14%)
  between operations  0.72 us (1%)
    pallas_call x1, Pallas kernels, on_device(): pl.pallas_call(exchange_kernel, out_shape=(jax.ShapeDtypeStruct((PEERS, 1...  39.5 us
    unnamed x27, local copies, waits for them, and re-layouts  6.92 us
    pallas_call x1, Pallas kernels, on_device(): pl.pallas_call(update_kernel, out_shape=(flat,) * 4, in_specs=[vmem] * 8,...  1.4 us

profile of v1, /device:TPU:1, one launch (start us, length us, event | category | flops | bytes accessed | tf_op | source)
XLA Modules:
  0.0 48.5 jit_solution(16087455803877150060)
XLA Ops:
  0.6 0.0 copy-start
  0.6 0.0 copy-start.5
  0.7 0.0 copy-start.10
  0.7 0.8 %copy.19.send_slots = s32[128,32]{1,0:T(8,128)S(1)} copy(s32[128,32]{0,1:T(8,128)} %param.21) | data formatting | bytes 32768 | tf_op args[7]
  1.5 0.0 copy-done
  1.5 0.0 copy-done.5
  1.5 0.0 copy-done.10
  1.5 0.0 copy-start.1
  1.5 0.8 %copy-done.1 = s32[8,2048]{1,0:T(8,128)S(1)} copy-done((s32[8,2048]{1,0:T(8,128)S(1)}, s32[8,2048]{1,0:T(8,128)}, u32[]{:S(2)}) %copy-start.1) | copy-done | bytes 65560
  2.4 0.0 copy-start.2
  2.4 0.8 %copy-done.2 = f32[3,4096]{1,0:T(4,128)S(1)} copy-done((f32[3,4096]{1,0:T(4,128)S(1)}, f32[3,4096]{1,0:T(4,128)}, u32[]{:S(2)}) %copy-start.2) | copy-done | bytes 49176
  3.2 0.0 copy-start.3
  3.2 0.8 %copy-done.3 = f32[3,4096]{1,0:T(4,128)S(1)} copy-done((f32[3,4096]{1,0:T(4,128)S(1)}, f32[3,4096]{1,0:T(4,128)}, u32[]{:S(2)}) %copy-start.3) | copy-done | bytes 49176
  4.1 0.0 copy-start.6
  4.1 0.7 %copy-done.6 = f32[4096]{0:T(1024)S(1)} copy-done((f32[4096]{0:T(1024)S(1)}, f32[4096]{0:T(1024)}, u32[]{:S(2)}) %copy-start.6) | copy-done | bytes 16408
  4.8 0.0 copy-start.7
  4.8 0.7 %copy-done.7 = f32[4096]{0:T(1024)S(1)} copy-done((f32[4096]{0:T(1024)S(1)}, f32[4096]{0:T(1024)}, u32[]{:S(2)}) %copy-start.7) | copy-done | bytes 16408
  5.5 0.7 %copy-done.8 = f32[4096]{0:T(1024)S(1)} copy-done((f32[4096]{0:T(1024)S(1)}, f32[4096]{0:T(1024)}, u32[]{:S(2)}) %copy-start.8) | copy-done | bytes 16408
  6.2 0.7 %copy-done.11 = f32[2048]{0:T(1024)S(1)} copy-done((f32[2048]{0:T(1024)S(1)}, f32[2048]{0:T(1024)}, u32[]{:S(2)}) %copy-start.11) | copy-done | bytes 8216
  6.9 0.7 %copy-done.12 = s32[2048]{0:T(1024)S(1)} copy-done((s32[2048]{0:T(1024)S(1)}, s32[2048]{0:T(1024)}, u32[]{:S(2)}) %copy-start.12) | copy-done | bytes 8216
  7.6 39.5 %exchange.1 = (f32[128,1,128]{2,1,0:T(1,128)S(1)}, f32[3,32,128]{2,1,0:T(8,128)S(1)}, f32[3,32,128]{2,1,0:T(8,128)S(1)}, f32[3,32,128]{2,1,0:T(8,128)S(1)}) custom-call(f32[3,4096]{1,0:T(4,128)S(1)} %copy-done, s32[8,2048]{1,0:T(8,128)S(1)} %copy-done.1, f32[1,2048]{1,0:T(1,128)S(1)} %bitcast.12, s32[1,2048]{1,0:T(1,128)S(1)} %bitcast.13, ...), custom_call_target="tpu_custom_call" | custom-call | tf_op jit(solution)/shard_map/exchange/pallas_call | solution.py:446
  47.1 0.0 copy-done.4
  47.1 0.0 copy-done.9
  47.1 1.4 %update.1 = (f32[3,4096]{1,0:T(4,128)}, f32[3,4096]{1,0:T(4,128)}, f32[3,4096]{1,0:T(4,128)}, f32[3,4096]{1,0:T(4,128)}) custom-call(f32[3,4096]{1,0:T(4,128)S(1)} %copy-done, f32[3,4096]{1,0:T(4,128)S(1)} %copy-done.4, f32[32,128]{1,0:T(8,128)S(1)} %bitcast.11, s32[128,32]{1,0:T(8,128)S(1)} %copy.19.send_slots, ...), custom_call_target="tpu_custom_call" | custom-call | tf_op jit(solution)/shard_map/update/pallas_call | solution.py:487
  (5 shorter events, 0.0 us)
Async XLA Ops:
  0.6 0.9 %copy-start = (f32[3,4096]{1,0:T(4,128)S(1)}, f32[3,4096]{1,0:T(4,128)}, u32[]{:S(2)}) copy-start(f32[3,4096]{1,0:T(4,128)} %disp.3) | copy-start | bytes 147460
  0.6 0.9 %copy-start.5 = (s32[4096]{0:T(1024)S(1)}, s32[4096]{0:T(1024)}, u32[]{:S(2)}) copy-start(s32[4096]{0:T(1024)} %param.22) | copy-start | bytes 49156
  0.7 0.9 %copy-start.10 = (f32[24,24]{1,0:T(8,128)S(1)}, f32[24,24]{1,0:T(8,128)}, u32[]{:S(2)}) copy-start(f32[24,24]{1,0:T(8,128)} %stiffness.1) | copy-start | bytes 6916
  1.5 0.8 %copy-start.1 = (s32[8,2048]{1,0:T(8,128)S(1)}, s32[8,2048]{1,0:T(8,128)}, u32[]{:S(2)}) copy-start(s32[8,2048]{1,0:T(8,128)} %hex_nodes.1) | copy-start | bytes 196612
  2.4 0.8 %copy-start.2 = (f32[3,4096]{1,0:T(4,128)S(1)}, f32[3,4096]{1,0:T(4,128)}, u32[]{:S(2)}) copy-start(f32[3,4096]{1,0:T(4,128)} %fine_disp.1) | copy-start | bytes 147460
  3.2 0.8 %copy-start.3 = (f32[3,4096]{1,0:T(4,128)S(1)}, f32[3,4096]{1,0:T(4,128)}, u32[]{:S(2)}) copy-start(f32[3,4096]{1,0:T(4,128)} %fine_velo.1) | copy-start | bytes 147460
  4.1 0.7 %copy-start.6 = (f32[4096]{0:T(1024)S(1)}, f32[4096]{0:T(1024)}, u32[]{:S(2)}) copy-start(f32[4096]{0:T(1024)} %param.25) | copy-start | bytes 49156
  4.8 0.7 %copy-start.7 = (f32[4096]{0:T(1024)S(1)}, f32[4096]{0:T(1024)}, u32[]{:S(2)}) copy-start(f32[4096]{0:T(1024)} %param.26) | copy-start | bytes 49156
  5.5 0.7 %copy-start.8 = (f32[4096]{0:T(1024)S(1)}, f32[4096]{0:T(1024)}, u32[]{:S(2)}) copy-start(f32[4096]{0:T(1024)} %param.27) | copy-start | bytes 49156
  6.2 0.7 %copy-start.11 = (f32[2048]{0:T(1024)S(1)}, f32[2048]{0:T(1024)}, u32[]{:S(2)}) copy-start(f32[2048]{0:T(1024)} %param.18) | copy-start | bytes 24580
  6.9 0.7 %copy-start.12 = (s32[2048]{0:T(1024)S(1)}, s32[2048]{0:T(1024)}, u32[]{:S(2)}) copy-start(s32[2048]{0:T(1024)} %param.19) | copy-start | bytes 24580
  7.6 39.5 %copy-start.4 = (f32[3,4096]{1,0:T(4,128)S(1)}, f32[3,4096]{1,0:T(4,128)}, u32[]{:S(2)}) copy-start(f32[3,4096]{1,0:T(4,128)} %velo.1) | copy-start | bytes 147460
  7.6 39.5 %copy-start.9 = (f32[4096]{0:T(1024)S(1)}, f32[4096]{0:T(1024)}, u32[]{:S(2)}) copy-start(f32[4096]{0:T(1024)} %param.16) | copy-start | bytes 49156

commit v2 on v1

v2 whole, which is shorter than its diff:
```python
import jax
import jax.numpy as jnp
from jax import lax
from jax.experimental import pallas as pl
from jax.experimental.pallas import tpu as pltpu
from jax.sharding import PartitionSpec as P

SUBSTEPS = 8
DT_FINE = 0.5
DT_COARSE = 1.0
PLASTIC = 0.3

LANES = 128
CAP = 32
PEERS = 128
RING = 8
ROWS = 32
RIM = 8
EXT = ROWS + 2 * RIM
ELEMS = 2048
CHUNK = 512
EDGE = 8
MESH = pl.DeviceIdType.MESH
F32 = jnp.float32
BF16 = jnp.bfloat16


def lane_lookup(acc, table_row, rows, row_idx, lane_idx):
    acc = list(acc)
    for r in rows:
        hit = row_idx == r
        for c in range(3):
            entry = jnp.broadcast_to(table_row(c, r), (8, LANES))
            found = jnp.take_along_axis(entry, lane_idx, axis=1, mode="promise_in_bounds")
            acc[c] = jnp.where(hit, found, acc[c])
    return acc


def scatter_terms(height, row_idx, lane_idx, values):
    n = row_idx.shape[1]
    row_hit = row_idx == lax.broadcasted_iota(jnp.int32, (height, n), 0)
    lane_hit = lane_idx == lax.broadcasted_iota(jnp.int32, (LANES, n), 0)
    parts = []
    for v in values:
        upper = v.astype(BF16).astype(F32)
        for part in (upper, v - upper):
            parts.append(jnp.where(row_hit, jnp.broadcast_to(part, (height, n)), 0.0))
    left = jnp.concatenate(parts, axis=0).astype(BF16)
    right = jnp.where(lane_hit, 1.0, 0.0).astype(BF16)
    return lax.dot_general(left, right, (((1,), (1,)), ((), ())), preferred_element_type=F32)


def flat(x, q):
    return jnp.concatenate([x[q + i : q + i + 1] for i in range(4)], axis=1)


def joined(sums, height):
    return [
        sums[2 * c * height : (2 * c + 1) * height] + sums[(2 * c + 1) * height : (2 * c + 2) * height] for c in range(3)
    ]


def by_slot(parts):
    stacked = jnp.concatenate([*parts, jnp.zeros((LANES - 3 * CAP, PEERS), F32)], axis=0)
    return jnp.transpose(stacked).reshape(PEERS, 1, LANES)


def split_rows(ref, store):
    for q in range(ROWS):
        for c in range(3):
            store(c, q, ref[c : c + 1, q * LANES : (q + 1) * LANES])


def substeps(pos, vel, total, shifted, attached, inv_mass, stiff, tie):
    for _ in range(SUBSTEPS):
        for c in range(len(pos)):
            before, after = shifted(pos[c])
            laplace = after - 2.0 * pos[c] + before
            accel = inv_mass * (stiff * laplace + tie * (attached[c] - pos[c]))
            vel[c] = vel[c] + DT_FINE * accel
            pos[c] = pos[c] + DT_FINE * vel[c]
            total[c] = total[c] + pos[c]


def exchange_kernel(
    disp_arg,
    send_slots_arg,
    fine_disp_arg,
    fine_velo_arg,
    fine_inv_mass_arg,
    fine_stiff_arg,
    tie_stiff_arg,
    hex_nodes_arg,
    fine_slot_arg,
    modulus_arg,
    yielded_arg,
    stiffness_arg,
    returned,
    internal,
    pos_out,
    vel_out,
    disp,
    send_slots,
    fine_disp,
    fine_velo,
    fine_inv_mass,
    fine_stiff,
    tie_stiff,
    hex_nodes,
    fine_slot,
    modulus,
    yielded,
    stiffness,
    ext,
    corner,
    force,
    force_in,
    picked,
    received,
    table,
    outgoing,
    edge_out,
    edge_in,
    tied_out,
    tied_in,
    a2a_send,
    a2a_recv,
    halo_send,
    halo_recv,
    load_sem,
):
    loads = [
        pltpu.make_async_copy(src, dst, load_sem.at[i])
        for i, (src, dst) in enumerate(
            (
                (disp_arg, disp),
                (send_slots_arg, send_slots),
                (fine_disp_arg, fine_disp),
                (fine_velo_arg, fine_velo),
                (fine_inv_mass_arg, fine_inv_mass),
                (fine_stiff_arg, fine_stiff),
                (tie_stiff_arg, tie_stiff),
                (hex_nodes_arg, hex_nodes),
                (fine_slot_arg, fine_slot),
                (modulus_arg, modulus),
                (yielded_arg, yielded),
                (stiffness_arg, stiffness),
            )
        )
    ]
    for load in loads:
        load.start()
    me, sub = lax.axis_index("mesh"), lax.axis_index("sub")
    n_sub = lax.axis_size("sub")
    top = sub == n_sub - 1
    low = sub == 0
    after = (jnp.where(top, lax.rem(me + 1, PEERS), me), jnp.where(top, 0, sub + 1))
    before = (jnp.where(low, lax.rem(me + PEERS - 1, PEERS), me), jnp.where(low, n_sub - 1, sub - 1))

    barrier = pltpu.get_barrier_semaphore()

    y, z, core = me // (2 * RING), lax.rem(me // 2, RING), lax.rem(me, 2)
    y_at = [lax.rem(y + i, RING) * (2 * RING) for i in range(RING)]
    z_at = [lax.rem(z + i, RING) * 2 for i in range(RING)]
    core_at = [core, 1 - core]
    hops = lambda i: min(i, RING - i)
    steps = [(dy, dz, dc) for dy in range(RING) for dz in range(RING) for dc in range(2) if (dy, dz, dc) != (0, 0, 0)]
    steps.sort(key=lambda step: -(2 * (hops(step[0]) + hops(step[1])) + step[2]))
    peers = [y_at[dy] + z_at[dz] + core_at[dc] for dy, dz, dc in steps]

    for neighbour in (before, after):
        pl.semaphore_signal(barrier, inc=1, device_id=neighbour, device_id_type=MESH)
    for peer in peers:
        pl.semaphore_signal(barrier, inc=1, device_id=(peer, sub), device_id_type=MESH)

    def to(neighbour, src, dst, which):
        return pltpu.make_async_remote_copy(
            src, dst, halo_send.at[which], halo_recv.at[which], device_id=neighbour, device_id_type=MESH
        )

    def put_disp(c, q, row):
        ext[c, RIM + q : RIM + q + 1, :] = row

    for load in loads[:2]:
        load.wait()
    split_rows(disp, put_disp)

    zero = jnp.zeros((8, LANES), F32)
    found = []
    for b in range(CAP // 8):
        at = send_slots[b * 8 : (b + 1) * 8]
        found.append(
            lane_lookup(
                [zero] * 3, lambda c, r: ext[c, RIM + r : RIM + r + 1, :], range(ROWS), at >> 7, at & (LANES - 1)
            )
        )
    picked[...] = by_slot([jnp.concatenate([f[c] for f in found], axis=0) for c in range(3)])

    def put_pos(c, q, row):
        pos_out[c, q : q + 1, :] = row

    def put_vel(c, q, row):
        vel_out[c, q : q + 1, :] = row

    for load in loads[2:7]:
        load.wait()
    split_rows(fine_disp, put_pos)
    split_rows(fine_velo, put_vel)
    for side, q in ((0, 0), (1, ROWS - 1)):
        for c in range(3):
            edge_out[side, c : c + 1, :] = pos_out[c, q : q + 1, :]
            edge_out[side, 3 + c : 4 + c, :] = vel_out[c, q : q + 1, :]
        edge_out[side, 6:7, :] = fine_inv_mass[q : q + 1, :]
        edge_out[side, 7:8, :] = fine_stiff[q : q + 1, :]
        edge_out[side, 8:9, :] = tie_stiff[q : q + 1, :]
        edge_out[side, 9:16, :] = jnp.zeros((7, LANES), F32)

    for load in loads[7:]:
        load.wait()

    def own_corner(t, carry):
        cols = pl.ds(pl.multiple_of(t * LANES, LANES), LANES)
        at = hex_nodes[:, cols] + RIM * LANES
        zero = jnp.zeros((8, LANES), F32)
        got = lane_lookup(
            [zero] * 3, lambda c, r: ext[c, r : r + 1, :], range(RIM, RIM + ROWS), at >> 7, at & (LANES - 1)
        )
        for c in range(3):
            corner[c * 8 : (c + 1) * 8, cols] = got[c]
        return carry

    lax.fori_loop(0, ELEMS // LANES, own_corner, 0)

    pl.semaphore_wait(barrier, PEERS + 1)

    halos = [
        to(after, ext.at[:, pl.ds(ROWS, RIM), :], ext.at[:, pl.ds(0, RIM), :], 0),
        to(before, ext.at[:, pl.ds(RIM, RIM), :], ext.at[:, pl.ds(RIM + ROWS, RIM), :], 1),
        to(before, edge_out.at[0], edge_in.at[1], 2),
        to(after, edge_out.at[1], edge_in.at[0], 3),
    ]
    for copy in halos[:2]:
        copy.start()

    def all_to_all(src, dst, which):
        for peer in peers:
            pltpu.make_async_remote_copy(
                src.at[peer],
                dst.at[me],
                a2a_send.at[which],
                a2a_recv.at[which],
                device_id=(peer, sub),
                device_id_type=MESH,
            ).start()
        dst[pl.ds(me, 1)] = src[pl.ds(me, 1)]
        return pltpu.make_async_remote_copy(
            src.at[pl.ds(0, PEERS - 1)],
            dst.at[pl.ds(0, PEERS - 1)],
            a2a_send.at[which],
            a2a_recv.at[which],
            device_id=after,
            device_id_type=MESH,
        )

    first = all_to_all(picked, received, 0)
    for copy in halos[2:]:
        copy.start()

    force[...] = jnp.zeros_like(force)
    for copy in halos[:2]:
        copy.wait()

    def rim_corner(t, carry):
        cols = pl.ds(pl.multiple_of(t * LANES, LANES), LANES)
        at = hex_nodes[:, cols] + RIM * LANES
        got = lane_lookup(
            [corner[c * 8 : (c + 1) * 8, cols] for c in range(3)],
            lambda c, r: ext[c, r : r + 1, :],
            [*range(RIM), *range(RIM + ROWS, EXT)],
            at >> 7,
            at & (LANES - 1),
        )
        for c in range(3):
            corner[c * 8 : (c + 1) * 8, cols] = got[c]
        return carry

    lax.fori_loop(0, ELEMS // LANES, rim_corner, 0)

    def element_force(t, carry):
        cols = pl.ds(pl.multiple_of(t * CHUNK, CHUNK), CHUNK)
        factor = modulus[:, cols] * jnp.where(yielded[:, cols] == 1, PLASTIC, 1.0)
        element = (
            jnp.dot(stiffness[...], corner[:, cols], precision=lax.Precision.HIGHEST, preferred_element_type=F32)
            * factor
        )
        at = hex_nodes[:, cols] + RIM * LANES
        row_at, lane_at = at >> 7, at & (LANES - 1)
        for k in range(8):
            force[...] += scatter_terms(
                EXT, row_at[k : k + 1], lane_at[k : k + 1], [element[c * 8 + k : c * 8 + k + 1] for c in range(3)]
            )
        return carry

    first.wait_recv()
    table[...] = jnp.transpose(received[...].reshape(PEERS, LANES))
    slot = fine_slot[...]
    row_at, lane_at = slot & (CAP - 1), slot >> 5
    blocks = []
    for b in range(ROWS // 8):
        zero = jnp.zeros((8, LANES), F32)
        blocks.append(
            lane_lookup(
                [zero] * 3,
                lambda c, r: table[c * CAP + r : c * CAP + r + 1, :],
                range(CAP),
                row_at[b * 8 : (b + 1) * 8],
                lane_at[b * 8 : (b + 1) * 8],
            )
        )
    attached = [jnp.concatenate([b[c] for b in blocks], axis=0) for c in range(3)]
    none = jnp.zeros((5, LANES), F32)
    tied_out[0] = jnp.concatenate([a[:1] for a in attached] + [none], axis=0)
    tied_out[1] = jnp.concatenate([a[ROWS - 1 :] for a in attached] + [none], axis=0)
    ties = [to(before, tied_out.at[0], tied_in.at[1], 6), to(after, tied_out.at[1], tied_in.at[0], 7)]
    for copy in ties:
        copy.start()

    lane = lax.broadcasted_iota(jnp.int32, (ROWS, LANES), 1)

    def shifted(x):
        right = pltpu.roll(x, 1, 1)
        left = pltpu.roll(x, LANES - 1, 1)
        prev = jnp.where(lane == 0, pltpu.roll(right, 1, 0), right)
        nxt = jnp.where(lane == LANES - 1, pltpu.roll(left, ROWS - 1, 0), left)
        return prev, nxt

    pos = [pos_out[c] for c in range(3)]
    vel = [vel_out[c] for c in range(3)]
    total = [jnp.zeros((ROWS, LANES), F32) for _ in range(3)]
    im, st, tie = fine_inv_mass[...], fine_stiff[...], tie_stiff[...]
    first_rows = [x[:1] for x in pos + vel + [im, st, tie] + attached]
    last_rows = [x[ROWS - 1 :] for x in pos + vel + [im, st, tie] + attached]
    substeps(pos, vel, total, shifted, attached, im, st, tie)

    sub_row = lax.broadcasted_iota(jnp.int32, (ROWS, LANES), 0)
    at_head = (sub_row == 0) & (lane < EDGE)
    at_tail = (sub_row == ROWS - 1) & (lane >= LANES - EDGE)
    at_ends = at_head | at_tail

    def tie_force(sum_of_pos):
        return [tie * (sum_of_pos[c] * (1.0 / SUBSTEPS) - attached[c]) for c in range(3)]

    pull = [jnp.where(at_ends, 0.0, p) for p in tie_force(total)]
    sums = None
    for q in range(0, ROWS, 4):
        term = scatter_terms(CAP, flat(row_at, q), flat(lane_at, q), [flat(p, q) for p in pull])
        sums = term if sums is None else sums + term

    lax.fori_loop(0, 2, element_force, 0)
    for copy in halos[2:] + ties:
        copy.wait()
    strip_lane = lax.broadcasted_iota(jnp.int32, (1, LANES), 1)
    starts = (me == 0) & (sub == 0)
    ends = (me == PEERS - 1) & (sub == n_sub - 1)

    def head(row, ghost):
        ghost = jnp.where(starts, 0.0, pltpu.roll(ghost, EDGE, 1))
        return jnp.where(strip_lane < EDGE, ghost, pltpu.roll(row, EDGE, 1))

    def tail(row, ghost):
        ghost = jnp.where(ends, 0.0, pltpu.roll(ghost, LANES - EDGE, 1))
        return jnp.where(strip_lane >= LANES - EDGE, ghost, pltpu.roll(row, LANES - EDGE, 1))

    ghost_head = [edge_in[0, i : i + 1, :] for i in range(9)] + [tied_in[0, c : c + 1, :] for c in range(3)]
    ghost_tail = [edge_in[1, i : i + 1, :] for i in range(9)] + [tied_in[1, c : c + 1, :] for c in range(3)]
    heads = [head(r, g) for r, g in zip(first_rows, ghost_head)]
    tails = [tail(r, g) for r, g in zip(last_rows, ghost_tail)]
    blank = jnp.zeros((2, LANES), F32)

    def strip(picks):
        return jnp.concatenate([heads[i] for i in picks] + [tails[i] for i in picks] + [blank], axis=0)

    strip_pos, strip_vel, strip_total = [strip((0, 1, 2))], [strip((3, 4, 5))], [jnp.zeros((8, LANES), F32)]
    substeps(
        strip_pos,
        strip_vel,
        strip_total,
        lambda x: (pltpu.roll(x, 1, 1), pltpu.roll(x, LANES - 1, 1)),
        [strip((9, 10, 11))],
        strip((6, 6, 6)),
        strip((7, 7, 7)),
        strip((8, 8, 8)),
    )
    def put_ends(whole, strips):
        forward = pltpu.roll(strips, LANES - EDGE, 1)
        back = pltpu.roll(strips, EDGE, 1)
        out = []
        for c in range(3):
            x = jnp.where(at_head, jnp.broadcast_to(forward[c : c + 1], (ROWS, LANES)), whole[c])
            out.append(jnp.where(at_tail, jnp.broadcast_to(back[3 + c : 4 + c], (ROWS, LANES)), x))
        return out

    pos = put_ends(pos, strip_pos[0])
    vel = put_ends(vel, strip_vel[0])
    total = put_ends(total, strip_total[0])
    end_pull = [jnp.where(at_ends, p, 0.0) for p in tie_force(total)]
    ends_of = lambda x: jnp.concatenate([x[:1], x[ROWS - 1 :]], axis=1)
    sums = sums + scatter_terms(CAP, ends_of(row_at), ends_of(lane_at), [ends_of(p) for p in end_pull])
    outgoing[...] = by_slot(joined(sums, CAP))
    second = all_to_all(outgoing, returned, 1)
    lax.fori_loop(2, 4, element_force, 0)
    for c in range(3):
        ext_force = force[2 * c * EXT : (2 * c + 1) * EXT, :] + force[(2 * c + 1) * EXT : (2 * c + 2) * EXT, :]
        force[2 * c * EXT : (2 * c + 1) * EXT, :] = ext_force
        force_in[2, c] = ext_force[:RIM]
        force_in[3, c] = ext_force[RIM + ROWS :]
    rims = [
        to(before, force_in.at[2], force_in.at[1], 4),
        to(after, force_in.at[3], force_in.at[0], 5),
    ]
    for copy in rims:
        copy.start()


    for c in range(3):
        pos_out[c] = pos[c]
        vel_out[c] = vel[c]
    for copy in rims:
        copy.wait()
    for c in range(3):
        own = force[2 * c * EXT + RIM : 2 * c * EXT + RIM + ROWS, :]
        internal[c, :RIM] = own[:RIM] + force_in[0, c]
        internal[c, RIM : ROWS - RIM] = own[RIM : ROWS - RIM]
        internal[c, ROWS - RIM :] = own[ROWS - RIM :] + force_in[1, c]
    first.wait_send()
    second.wait()


def update_kernel(
    disp, velo, inv_mass, send_slots, returned, internal, pos, vel, disp_new, velo_new, pos_out, vel_out
):
    slot_at = send_slots[...]
    back = jnp.transpose(returned[...].reshape(PEERS, LANES))
    back = [back[c * CAP : (c + 1) * CAP] for c in range(3)]
    row_at, lane_at = slot_at >> 7, slot_at & (LANES - 1)
    sums = None
    for q in range(0, CAP, 4):
        term = scatter_terms(ROWS, flat(row_at, q), flat(lane_at, q), [flat(b, q) for b in back])
        sums = term if sums is None else sums + term
    change = [inv_mass[...] * (coupling - internal[c]) for c, coupling in enumerate(joined(sums, ROWS))]
    for q in range(ROWS):
        cols = slice(q * LANES, (q + 1) * LANES)

        def three(x):
            return jnp.concatenate([x(c) for c in range(3)], axis=0)

        v = velo[:, cols] + DT_COARSE * three(lambda c: change[c][q : q + 1])
        velo_new[:, cols] = v
        disp_new[:, cols] = disp[:, cols] + DT_COARSE * v
        pos_out[:, cols] = three(lambda c: pos[c, q : q + 1, :])
        vel_out[:, cols] = three(lambda c: vel[c, q : q + 1, :])


def on_device(
    disp,
    velo,
    inv_mass,
    hex_nodes,
    modulus,
    yielded,
    stiffness,
    send_slots,
    fine_slot,
    fine_disp,
    fine_velo,
    fine_inv_mass,
    fine_stiff,
    tie_stiff,
):
    vmem = pl.BlockSpec(memory_space=pltpu.VMEM)
    chain = jax.ShapeDtypeStruct((3, ROWS, LANES), F32)
    flat = jax.ShapeDtypeStruct(disp.shape, F32)
    rows = lambda x: x.reshape(ROWS, LANES)
    line = lambda x: x.reshape(1, ELEMS)
    buffer = lambda *shape: pltpu.VMEM(shape, F32)
    slots = send_slots.T
    loaded = (
        disp,
        slots,
        fine_disp,
        fine_velo,
        rows(fine_inv_mass),
        rows(fine_stiff),
        rows(tie_stiff),
        hex_nodes,
        rows(fine_slot),
        line(modulus),
        line(yielded),
        stiffness,
    )
    returned, internal, pos, vel = pl.pallas_call(
        exchange_kernel,
        out_shape=(jax.ShapeDtypeStruct((PEERS, 1, LANES), F32), chain, chain, chain),
        in_specs=[pl.BlockSpec(memory_space=pltpu.HBM)] * 12,
        out_specs=(vmem,) * 4,
        scratch_shapes=[
            *[pltpu.VMEM(x.shape, x.dtype) for x in loaded],
            buffer(3, EXT, LANES),
            buffer(24, ELEMS),
            buffer(6 * EXT, LANES),
            buffer(4, 3, RIM, LANES),
            buffer(PEERS, 1, LANES),
            buffer(PEERS, 1, LANES),
            buffer(LANES, PEERS),
            buffer(PEERS, 1, LANES),
            buffer(2, 16, LANES),
            buffer(2, 16, LANES),
            buffer(2, 8, LANES),
            buffer(2, 8, LANES),
            pltpu.SemaphoreType.DMA((2,)),
            pltpu.SemaphoreType.DMA((2,)),
            pltpu.SemaphoreType.DMA((8,)),
            pltpu.SemaphoreType.DMA((8,)),
            pltpu.SemaphoreType.DMA((len(loaded),)),
        ],
        compiler_params=pltpu.CompilerParams(
            collective_id=0, has_side_effects=True, vmem_limit_bytes=32 * 1024 * 1024
        ),
        name="exchange",
    )(*[pltpu.with_memory_space_constraint(x, pltpu.HBM) for x in loaded])
    return pl.pallas_call(
        update_kernel,
        out_shape=(flat,) * 4,
        in_specs=[vmem] * 8,
        out_specs=(vmem,) * 4,
        compiler_params=pltpu.CompilerParams(vmem_limit_bytes=32 * 1024 * 1024),
        name="update",
    )(disp, velo, rows(inv_mass), slots, returned, internal, pos, vel)


def solution(mesh):
    placed = (
        P(None, ("mesh", "sub")),
        P(None, ("mesh", "sub")),
        P(("mesh", "sub")),
        P(None, ("mesh", "sub")),
        P(("mesh", "sub")),
        P(("mesh", "sub")),
        P(),
        P(("mesh", "sub"), None),
        P(("mesh", "sub")),
        P(None, ("mesh", "sub")),
        P(None, ("mesh", "sub")),
        P(("mesh", "sub")),
        P(("mesh", "sub")),
        P(("mesh", "sub")),
    )
    return jax.shard_map(
        on_device,
        mesh=mesh,
        in_specs=placed,
        out_specs=(
            P(None, ("mesh", "sub")),
            P(None, ("mesh", "sub")),
            P(None, ("mesh", "sub")),
            P(None, ("mesh", "sub")),
        ),
        check_vma=False,
    )
```

time: 49.1 us -> 38.3 us (0.78)
  local copies, waits for them, and re-layouts: 6.92 us -> 0.02 us
  Pallas kernels: 40.9 us -> 37.4 us
    unnamed x27 -> x8, local copies, waits for them, and re-layouts: 6.92 us -> 0.02 us
    pallas_call x1, Pallas kernels: 39.5 us -> 36.1 us  [on_device(): pl.pallas_call(exchange_kernel, out_shape=(jax.ShapeDtypeStruct((PEERS, 1...]
where the time goes in v2:
time: 38.3 us; the launch traced here: 38.1 us
  Pallas kernels  37.4 us (98%)
  between operations  0.71 us (2%)
    pallas_call x1, Pallas kernels, on_device(): pl.pallas_call(exchange_kernel, out_shape=(jax.ShapeDtypeStruct((PEERS, 1...  36.1 us
    pallas_call x1, Pallas kernels, on_device(): pl.pallas_call(update_kernel, out_shape=(flat,) * 4, in_specs=[vmem] * 8,...  1.37 us

profile of v2, /device:TPU:1, one launch (start us, length us, event | category | flops | bytes accessed | tf_op | source)
XLA Modules:
  0.0 38.1 jit_solution(16232560551013669844)
XLA Ops:
  0.6 0.0 copy-start
  0.6 0.0 copy-start.1
  0.7 0.0 copy-start.2
  0.7 0.0 copy-start.3
  0.7 36.1 %exchange.1 = (f32[128,1,128]{2,1,0:T(1,128)S(1)}, f32[3,32,128]{2,1,0:T(8,128)S(1)}, f32[3,32,128]{2,1,0:T(8,128)S(1)}, f32[3,32,128]{2,1,0:T(8,128)S(1)}) custom-call(f32[3,4096]{1,0:T(4,128)} %disp.1, s32[32,128]{1,0:T(8,128)} %bitcast.8, f32[3,4096]{1,0:T(4,128)} %fine_disp_arg.1, f32[3,4096]{1,0:T(4,128)} %fine_velo_arg.1, f32[32,128]{1,0:T(8,128)} %bitcast.11, ...), custom_call_target="tpu_custom_call" | custom-call | tf_op jit(solution)/shard_map/exchange/pallas_call | solution.py:501
  36.7 0.0 copy-done
  36.7 0.0 copy-done.1
  36.8 0.0 copy-done.2
  36.8 0.0 copy-done.3
  36.8 1.4 %update.1 = (f32[3,4096]{1,0:T(4,128)}, f32[3,4096]{1,0:T(4,128)}, f32[3,4096]{1,0:T(4,128)}, f32[3,4096]{1,0:T(4,128)}) custom-call(f32[3,4096]{1,0:T(4,128)S(1)} %copy-done, f32[3,4096]{1,0:T(4,128)S(1)} %copy-done.2, f32[32,128]{1,0:T(8,128)S(1)} %bitcast.10, s32[32,128]{1,0:T(8,128)S(1)} %bitcast.9, f32[128,1,128]{2,1,0:T(1,128)S(1)} %get-tuple-element.8.returned, ...), custom_call_target="tpu_custom_call" | custom-call | tf_op jit(solution)/shard_map/update/pallas_call | solution.py:531
Async XLA Ops:
  0.6 36.1 %copy-start = (f32[3,4096]{1,0:T(4,128)S(1)}, f32[3,4096]{1,0:T(4,128)}, u32[]{:S(2)}) copy-start(f32[3,4096]{1,0:T(4,128)} %disp.1) | copy-start | bytes 147460
  0.6 36.1 %copy-start.1 = (s32[128,32]{0,1:T(8,128)S(1)}, s32[128,32]{0,1:T(8,128)}, u32[]{:S(2)}) copy-start(s32[128,32]{0,1:T(8,128)} %param.21) | copy-start | bytes 49156
  0.7 36.1 %copy-start.2 = (f32[3,4096]{1,0:T(4,128)S(1)}, f32[3,4096]{1,0:T(4,128)}, u32[]{:S(2)}) copy-start(f32[3,4096]{1,0:T(4,128)} %velo.1) | copy-start | bytes 147460
  0.7 36.1 %copy-start.3 = (f32[4096]{0:T(1024)S(1)}, f32[4096]{0:T(1024)}, u32[]{:S(2)}) copy-start(f32[4096]{0:T(1024)} %param.16) | copy-start | bytes 49156

commit v3 on v2

--- a/solution.py
+++ b/solution.py
@@ -62,7 +62,7 @@
 
 def by_slot(parts):
     stacked = jnp.concatenate([*parts, jnp.zeros((LANES - 3 * CAP, PEERS), F32)], axis=0)
-    return jnp.transpose(stacked).reshape(PEERS, 1, LANES)
+    return jnp.transpose(stacked)
 
 
 def split_rows(ref, store):
@@ -97,8 +97,8 @@
     stiffness_arg,
     returned,
     internal,
-    pos_out,
-    vel_out,
+    pos_flat,
+    vel_flat,
     disp,
     send_slots,
     fine_disp,
@@ -111,6 +111,8 @@
     modulus,
     yielded,
     stiffness,
+    pos_out,
+    vel_out,
     ext,
     corner,
     force,
@@ -168,11 +170,10 @@
     steps.sort(key=lambda step: -(2 * (hops(step[0]) + hops(step[1])) + step[2]))
     peers = [y_at[dy] + z_at[dz] + core_at[dc] for dy, dz, dc in steps]
 
+    for peer in peers:
+        pl.semaphore_signal(barrier, inc=1, device_id=(peer, sub), device_id_type=MESH)
     for neighbour in (before, after):
         pl.semaphore_signal(barrier, inc=1, device_id=neighbour, device_id_type=MESH)
-    for peer in peers:
-        pl.semaphore_signal(barrier, inc=1, device_id=(peer, sub), device_id_type=MESH)
-
     def to(neighbour, src, dst, which):
         return pltpu.make_async_remote_copy(
             src, dst, halo_send.at[which], halo_recv.at[which], device_id=neighbour, device_id_type=MESH
@@ -218,19 +219,6 @@
     for load in loads[7:]:
         load.wait()
 
-    def own_corner(t, carry):
-        cols = pl.ds(pl.multiple_of(t * LANES, LANES), LANES)
-        at = hex_nodes[:, cols] + RIM * LANES
-        zero = jnp.zeros((8, LANES), F32)
-        got = lane_lookup(
-            [zero] * 3, lambda c, r: ext[c, r : r + 1, :], range(RIM, RIM + ROWS), at >> 7, at & (LANES - 1)
-        )
-        for c in range(3):
-            corner[c * 8 : (c + 1) * 8, cols] = got[c]
-        return carry
-
-    lax.fori_loop(0, ELEMS // LANES, own_corner, 0)
-
     pl.semaphore_wait(barrier, PEERS + 1)
 
     halos = [
@@ -243,15 +231,18 @@
         copy.start()
 
     def all_to_all(src, dst, which):
-        for peer in peers:
+        def send(peer):
             pltpu.make_async_remote_copy(
-                src.at[peer],
-                dst.at[me],
+                src.at[pl.ds(peer, 1)],
+                dst.at[pl.ds(me, 1)],
                 a2a_send.at[which],
                 a2a_recv.at[which],
                 device_id=(peer, sub),
                 device_id_type=MESH,
             ).start()
+
+        for peer in peers:
+            send(peer)
         dst[pl.ds(me, 1)] = src[pl.ds(me, 1)]
         return pltpu.make_async_remote_copy(
             src.at[pl.ds(0, PEERS - 1)],
@@ -266,7 +257,21 @@
     for copy in halos[2:]:
         copy.start()
 
+    def own_corner(t, carry):
+        cols = pl.ds(pl.multiple_of(t * LANES, LANES), LANES)
+        at = hex_nodes[:, cols] + RIM * LANES
+        zero = jnp.zeros((8, LANES), F32)
+        got = lane_lookup(
+            [zero] * 3, lambda c, r: ext[c, r : r + 1, :], range(RIM, RIM + ROWS), at >> 7, at & (LANES - 1)
+        )
+        for c in range(3):
+            corner[c * 8 : (c + 1) * 8, cols] = got[c]
+        return carry
+
+    lax.fori_loop(0, ELEMS // LANES, own_corner, 0)
+
     force[...] = jnp.zeros_like(force)
+    tied_out[...] = jnp.zeros_like(tied_out)
     for copy in halos[:2]:
         copy.wait()
 
@@ -302,28 +307,32 @@
         return carry
 
     first.wait_recv()
-    table[...] = jnp.transpose(received[...].reshape(PEERS, LANES))
+    table[...] = jnp.transpose(received[...])
     slot = fine_slot[...]
     row_at, lane_at = slot & (CAP - 1), slot >> 5
-    blocks = []
-    for b in range(ROWS // 8):
-        zero = jnp.zeros((8, LANES), F32)
-        blocks.append(
-            lane_lookup(
-                [zero] * 3,
-                lambda c, r: table[c * CAP + r : c * CAP + r + 1, :],
-                range(CAP),
-                row_at[b * 8 : (b + 1) * 8],
-                lane_at[b * 8 : (b + 1) * 8],
-            )
-        )
-    attached = [jnp.concatenate([b[c] for b in blocks], axis=0) for c in range(3)]
-    none = jnp.zeros((5, LANES), F32)
-    tied_out[0] = jnp.concatenate([a[:1] for a in attached] + [none], axis=0)
-    tied_out[1] = jnp.concatenate([a[ROWS - 1 :] for a in attached] + [none], axis=0)
+    zero = jnp.zeros((8, LANES), F32)
+
+    def lookup(rows, lanes):
+        return lane_lookup(
+            [zero] * 3, lambda c, r: table[c * CAP + r : c * CAP + r + 1, :], range(CAP), rows, lanes
+        )
+
+    def ends_first(x):
+        return jnp.concatenate([x[:4], x[ROWS - 4 :]], axis=0)
+
+    end_block = lookup(ends_first(row_at), ends_first(lane_at))
+    for c in range(3):
+        tied_out[0, 3 + c : 4 + c, :] = end_block[c][:1]
+        tied_out[1, c : c + 1, :] = end_block[c][7:]
     ties = [to(before, tied_out.at[0], tied_in.at[1], 6), to(after, tied_out.at[1], tied_in.at[0], 7)]
     for copy in ties:
         copy.start()
+    blocks = [
+        lookup(row_at[4 + b * 8 : 12 + b * 8], lane_at[4 + b * 8 : 12 + b * 8]) for b in range(ROWS // 8 - 1)
+    ]
+    attached = [
+        jnp.concatenate([end_block[c][:4]] + [b[c] for b in blocks] + [end_block[c][4:]], axis=0) for c in range(3)
+    ]
 
     lane = lax.broadcasted_iota(jnp.int32, (ROWS, LANES), 1)
 
@@ -356,8 +365,8 @@
         term = scatter_terms(CAP, flat(row_at, q), flat(lane_at, q), [flat(p, q) for p in pull])
         sums = term if sums is None else sums + term
 
-    lax.fori_loop(0, 2, element_force, 0)
-    for copy in halos[2:] + ties:
+    lax.fori_loop(0, 1, element_force, 0)
+    for copy in halos[2:]:
         copy.wait()
     strip_lane = lax.broadcasted_iota(jnp.int32, (1, LANES), 1)
     starts = (me == 0) & (sub == 0)
@@ -371,26 +380,40 @@
         ghost = jnp.where(ends, 0.0, pltpu.roll(ghost, LANES - EDGE, 1))
         return jnp.where(strip_lane >= LANES - EDGE, ghost, pltpu.roll(row, LANES - EDGE, 1))
 
-    ghost_head = [edge_in[0, i : i + 1, :] for i in range(9)] + [tied_in[0, c : c + 1, :] for c in range(3)]
-    ghost_tail = [edge_in[1, i : i + 1, :] for i in range(9)] + [tied_in[1, c : c + 1, :] for c in range(3)]
-    heads = [head(r, g) for r, g in zip(first_rows, ghost_head)]
-    tails = [tail(r, g) for r, g in zip(last_rows, ghost_tail)]
+    heads = [head(r, edge_in[0, i : i + 1, :]) for i, r in enumerate(first_rows[:9])]
+    tails = [tail(r, edge_in[1, i : i + 1, :]) for i, r in enumerate(last_rows[:9])]
     blank = jnp.zeros((2, LANES), F32)
 
     def strip(picks):
         return jnp.concatenate([heads[i] for i in picks] + [tails[i] for i in picks] + [blank], axis=0)
 
     strip_pos, strip_vel, strip_total = [strip((0, 1, 2))], [strip((3, 4, 5))], [jnp.zeros((8, LANES), F32)]
+    strip_im, strip_st, strip_tie = strip((6, 6, 6)), strip((7, 7, 7)), strip((8, 8, 8))
+    own_tied = jnp.concatenate(
+        [pltpu.roll(x, EDGE, 1) for x in first_rows[9:]] + [pltpu.roll(x, LANES - EDGE, 1) for x in last_rows[9:]] + [blank],
+        axis=0,
+    )
+    strip_row = lax.broadcasted_iota(jnp.int32, (8, LANES), 0)
+    ghost_lane = lax.broadcasted_iota(jnp.int32, (8, LANES), 1)
+    beyond = (starts & (strip_row < 3)) | (ends & (strip_row >= 3))
+    from_before = (strip_row < 3) & (ghost_lane < EDGE)
+    from_after = (strip_row >= 3) & (ghost_lane >= LANES - EDGE)
+    for copy in ties:
+        copy.wait()
+    strip_tied = jnp.where(from_before, pltpu.roll(tied_in[0], EDGE, 1), own_tied)
+    strip_tied = jnp.where(from_after, pltpu.roll(tied_in[1], LANES - EDGE, 1), strip_tied)
+    strip_tied = jnp.where(beyond & (from_before | from_after), 0.0, strip_tied)
     substeps(
         strip_pos,
         strip_vel,
         strip_total,
         lambda x: (pltpu.roll(x, 1, 1), pltpu.roll(x, LANES - 1, 1)),
-        [strip((9, 10, 11))],
-        strip((6, 6, 6)),
-        strip((7, 7, 7)),
-        strip((8, 8, 8)),
+        [strip_tied],
+        strip_im,
+        strip_st,
+        strip_tie,
     )
+
     def put_ends(whole, strips):
         forward = pltpu.roll(strips, LANES - EDGE, 1)
         back = pltpu.roll(strips, EDGE, 1)
@@ -408,7 +431,7 @@
     sums = sums + scatter_terms(CAP, ends_of(row_at), ends_of(lane_at), [ends_of(p) for p in end_pull])
     outgoing[...] = by_slot(joined(sums, CAP))
     second = all_to_all(outgoing, returned, 1)
-    lax.fori_loop(2, 4, element_force, 0)
+    lax.fori_loop(1, 4, element_force, 0)
     for c in range(3):
         ext_force = force[2 * c * EXT : (2 * c + 1) * EXT, :] + force[(2 * c + 1) * EXT : (2 * c + 2) * EXT, :]
         force[2 * c * EXT : (2 * c + 1) * EXT, :] = ext_force
@@ -422,9 +445,10 @@
         copy.start()
 
 
-    for c in range(3):
-        pos_out[c] = pos[c]
-        vel_out[c] = vel[c]
+    for q in range(ROWS):
+        cols = slice(q * LANES, (q + 1) * LANES)
+        pos_flat[:, cols] = jnp.concatenate([x[q : q + 1] for x in pos], axis=0)
+        vel_flat[:, cols] = jnp.concatenate([x[q : q + 1] for x in vel], axis=0)
     for copy in rims:
         copy.wait()
     for c in range(3):
@@ -437,10 +461,13 @@
 
 
 def update_kernel(
-    disp, velo, inv_mass, send_slots, returned, internal, pos, vel, disp_new, velo_new, pos_out, vel_out
+    disp, velo, inv_mass, send_slots, returned, internal, pos, vel, disp_new, velo_new, pos_out, vel_out, sem
 ):
+    out = [pltpu.make_async_copy(pos, pos_out, sem.at[0]), pltpu.make_async_copy(vel, vel_out, sem.at[1])]
+    for copy in out:
+        copy.start()
     slot_at = send_slots[...]
-    back = jnp.transpose(returned[...].reshape(PEERS, LANES))
+    back = jnp.transpose(returned[...])
     back = [back[c * CAP : (c + 1) * CAP] for c in range(3)]
     row_at, lane_at = slot_at >> 7, slot_at & (LANES - 1)
     sums = None
@@ -457,8 +484,8 @@
         v = velo[:, cols] + DT_COARSE * three(lambda c: change[c][q : q + 1])
         velo_new[:, cols] = v
         disp_new[:, cols] = disp[:, cols] + DT_COARSE * v
-        pos_out[:, cols] = three(lambda c: pos[c, q : q + 1, :])
-        vel_out[:, cols] = three(lambda c: vel[c, q : q + 1, :])
+    for copy in out:
+        copy.wait()
 
 
 def on_device(
@@ -479,7 +506,7 @@
 ):
     vmem = pl.BlockSpec(memory_space=pltpu.VMEM)
     chain = jax.ShapeDtypeStruct((3, ROWS, LANES), F32)
-    flat = jax.ShapeDtypeStruct(disp.shape, F32)
+    flat_shape = jax.ShapeDtypeStruct(disp.shape, F32)
     rows = lambda x: x.reshape(ROWS, LANES)
     line = lambda x: x.reshape(1, ELEMS)
     buffer = lambda *shape: pltpu.VMEM(shape, F32)
@@ -500,19 +527,21 @@
     )
     returned, internal, pos, vel = pl.pallas_call(
         exchange_kernel,
-        out_shape=(jax.ShapeDtypeStruct((PEERS, 1, LANES), F32), chain, chain, chain),
+        out_shape=(jax.ShapeDtypeStruct((PEERS, LANES), F32), chain, flat_shape, flat_shape),
         in_specs=[pl.BlockSpec(memory_space=pltpu.HBM)] * 12,
         out_specs=(vmem,) * 4,
         scratch_shapes=[
             *[pltpu.VMEM(x.shape, x.dtype) for x in loaded],
+            buffer(3, ROWS, LANES),
+            buffer(3, ROWS, LANES),
             buffer(3, EXT, LANES),
             buffer(24, ELEMS),
             buffer(6 * EXT, LANES),
             buffer(4, 3, RIM, LANES),
-            buffer(PEERS, 1, LANES),
-            buffer(PEERS, 1, LANES),
+            buffer(PEERS, LANES),
+            buffer(PEERS, LANES),
             buffer(LANES, PEERS),
-            buffer(PEERS, 1, LANES),
+            buffer(PEERS, LANES),
             buffer(2, 16, LANES),
             buffer(2, 16, LANES),
             buffer(2, 8, LANES),
@@ -530,9 +559,10 @@
     )(*[pltpu.with_memory_space_constraint(x, pltpu.HBM) for x in loaded])
     return pl.pallas_call(
         update_kernel,
-        out_shape=(flat,) * 4,
+        out_shape=(flat_shape,) * 4,
         in_specs=[vmem] * 8,
-        out_specs=(vmem,) * 4,
+        out_specs=(vmem, vmem, pl.BlockSpec(memory_space=pl.ANY), pl.BlockSpec(memory_space=pl.ANY)),
+        scratch_shapes=[pltpu.SemaphoreType.DMA((2,))],
         compiler_params=pltpu.CompilerParams(vmem_limit_bytes=32 * 1024 * 1024),
         name="update",
     )(disp, velo, rows(inv_mass), slots, returned, internal, pos, vel)

time: 38.3 us -> 37.9 us (0.990)
  Pallas kernels: 37.4 us -> 37 us
    pallas_call x2, Pallas kernels: 37.4 us -> 37 us  [the longest x1 35.7 us: on_device(): pl.pallas_call(exchange_kernel, out_shape=(jax.ShapeDtypeStruct((PEERS, L...]
where the time goes in v3:
time: 37.9 us; the launch traced here: 37.7 us
  Pallas kernels  37 us (98%)
  between operations  0.71 us (2%)
    pallas_call x1, Pallas kernels, on_device(): pl.pallas_call(exchange_kernel, out_shape=(jax.ShapeDtypeStruct((PEERS, L...  35.7 us
    pallas_call x1, Pallas kernels, on_device(): pl.pallas_call(update_kernel, out_shape=(flat_shape,) * 4, in_specs=[vmem...  1.34 us

profile of v3, /device:TPU:1, one launch (start us, length us, event | category | flops | bytes accessed | tf_op | source)
XLA Modules:
  0.0 37.7 jit_solution(477845372981037071)
XLA Ops:
  0.6 0.0 copy-start
  0.6 0.0 copy-start.1
  0.7 0.0 copy-start.2
  0.7 0.0 copy-start.3
  0.7 35.7 %exchange.1 = (f32[128,128]{1,0:T(8,128)S(1)}, f32[3,32,128]{2,1,0:T(8,128)S(1)}, f32[3,4096]{1,0:T(4,128)S(1)}, f32[3,4096]{1,0:T(4,128)S(1)}) custom-call(f32[3,4096]{1,0:T(4,128)} %disp.1, s32[32,128]{1,0:T(8,128)} %bitcast.8, f32[3,4096]{1,0:T(4,128)} %fine_disp_arg.1, f32[3,4096]{1,0:T(4,128)} %fine_velo_arg.1, f32[32,128]{1,0:T(8,128)} %bitcast.11, ...), custom_call_target="tpu_custom_call" | custom-call | tf_op jit(solution)/shard_map/exchange/pallas_call | solution.py:528
  36.4 0.0 copy-done
  36.4 0.0 copy-done.1
  36.4 0.0 copy-done.2
  36.4 0.0 copy-done.3
  36.4 1.3 %update.1 = (f32[3,4096]{1,0:T(4,128)}, f32[3,4096]{1,0:T(4,128)}, f32[3,4096]{1,0:T(4,128)}, f32[3,4096]{1,0:T(4,128)}) custom-call(f32[3,4096]{1,0:T(4,128)S(1)} %copy-done, f32[3,4096]{1,0:T(4,128)S(1)} %copy-done.1, f32[32,128]{1,0:T(8,128)S(1)} %bitcast.10, s32[32,128]{1,0:T(8,128)S(1)} %bitcast.9, f32[128,128]{1,0:T(8,128)S(1)} %get-tuple-element.8.returned, ...), custom_call_target="tpu_custom_call" | custom-call | tf_op jit(solution)/shard_map/update/pallas_call | solution.py:560
Async XLA Ops:
  0.6 35.7 %copy-start = (f32[3,4096]{1,0:T(4,128)S(1)}, f32[3,4096]{1,0:T(4,128)}, u32[]{:S(2)}) copy-start(f32[3,4096]{1,0:T(4,128)} %disp.1) | copy-start | bytes 147460
  0.6 35.7 %copy-start.1 = (f32[3,4096]{1,0:T(4,128)S(1)}, f32[3,4096]{1,0:T(4,128)}, u32[]{:S(2)}) copy-start(f32[3,4096]{1,0:T(4,128)} %velo.1) | copy-start | bytes 147460
  0.7 35.7 %copy-start.2 = (s32[128,32]{0,1:T(8,128)S(1)}, s32[128,32]{0,1:T(8,128)}, u32[]{:S(2)}) copy-start(s32[128,32]{0,1:T(8,128)} %param.21) | copy-start | bytes 49156
  0.7 35.7 %copy-start.3 = (f32[4096]{0:T(1024)S(1)}, f32[4096]{0:T(1024)}, u32[]{:S(2)}) copy-start(f32[4096]{0:T(1024)} %param.16) | copy-start | bytes 49156
